TPU v7x, 32 devices: a whole 2x2x4 slice. The times are simulated.
32 devices in a mesh: dp: 2 (over x), lat: 16 (over z, y, core).
Axes of the slice: x: 2, y: 2, z: 4, core: 2. Of those that a mesh axis runs over, the one named last changes fastest.
Arguments:
- states: bfloat16 [2, 64, 128, 128], P('dp', 'lat'), may hold values from -6 to 6
- basis_table: bfloat16 [64, 25, 9, 5], replicated, may hold values from -1.1953125 to 1.1953125
- offsets: int32 [64], replicated, may hold values from -12 to -8, as said below
- widths: int32 [64], replicated, may hold values from 21 to 25, as said below
- mixing: bfloat16 [9, 128, 128], replicated, may hold values from -0.1875 to 0.1875
- cotangent: bfloat16 [2, 64, 128, 128], P('dp', 'lat'), may hold values from -6 to 6
Outputs:
- output: bfloat16 [2, 64, 128, 128], P('dp', 'lat')
- grad_states: bfloat16 [2, 64, 128, 128], P('dp', 'lat')
- grad_mixing: float32 [9, 128, 128], replicated
Inputs may be any that keep to these rules, and one draw needn't show every extreme that they name: The support of every output latitude o contains o itself and lies within latitudes o - 12 to o + 12, so offsets[o] is at most 13 - widths[o]. widths is 25 at the two pole latitudes 0 and 63.
All inputs are finite; a program needn't handle non-finite values.
Results may differ from a plain program's by a relative error of at most 0.0049.
Values may be sent and summed in bfloat16 or wider, within the bound.
A program may use at most 64 MiB of HBM per device.

v0:
```python
import math

import jax
import jax.numpy as jnp
from jax import lax
from jax.sharding import PartitionSpec as P

TAPS = 5
HALO = 12


def shifted(x, axis, by):
    count = lax.axis_size(axis)
    pairs = [(i, i + by) for i in range(count) if 0 <= i + by < count]
    return lax.ppermute(x, axis, pairs)


def band_matrix(table_rows, offsets, widths, ext_rows, offset_base):
    out_rows = offsets.shape[0]
    support = table_rows.shape[1]
    slot_ids = jnp.arange(support, dtype=jnp.int32)
    target = (
        jnp.arange(out_rows, dtype=jnp.int32)[:, None]
        + offset_base
        + offsets[:, None]
        + slot_ids[None, :]
    )
    column = jnp.arange(ext_rows, dtype=jnp.int32)
    matches = (target[:, :, None] == column[None, None, :]) & (
        slot_ids[None, :, None] < widths[:, None, None]
    )
    return jnp.einsum(
        "qskt,qse->ktqe",
        table_rows,
        matches.astype(jnp.bfloat16),
        preferred_element_type=jnp.float32,
    ).astype(jnp.bfloat16)


def halo_rows(stacked, axis_rows):
    band_rows = stacked.shape[axis_rows]
    hop_count = -(-HALO // band_rows)
    above = []
    for distance in range(hop_count, 0, -1):
        row_count = min(band_rows, HALO - (distance - 1) * band_rows)
        piece = stacked
        above.append(shifted(piece, "lat", distance))
    below = []
    for distance in range(1, hop_count + 1):
        row_count = min(band_rows, HALO - (distance - 1) * band_rows)
        piece = stacked
        below.append(shifted(piece, "lat", -distance))
    return jnp.concatenate(above + [stacked] + below, axis=axis_rows)


def adjoint_rows(matrix, grad_filtered, half_taps):
    total = None
    for tap_index in range(TAPS):
        term = jnp.einsum(
            "kqe,bkqlc->belc",
            matrix[:, tap_index],
            grad_filtered,
            preferred_element_type=jnp.float32,
        )
        term = jnp.roll(term, tap_index - half_taps, axis=2)
        total = term if total is None else total + term
    return total


def shards(states, basis_table, offsets, widths, mixing, cotangent):
    band_rows = states.shape[1]
    half_taps = TAPS // 2
    ext_rows = band_rows + 2 * HALO
    first_row = lax.axis_index("lat") * band_rows
    table_rows = lax.dynamic_slice_in_dim(basis_table, first_row, band_rows, 0)
    own_offsets = lax.dynamic_slice_in_dim(offsets, first_row, band_rows, 0)
    own_widths = lax.dynamic_slice_in_dim(widths, first_row, band_rows, 0)
    both_ext = halo_rows(jnp.stack((states, cotangent)), 2)
    states_ext = both_ext[0]
    cot_ext = both_ext[1]
    forward_matrix = band_matrix(table_rows, own_offsets, own_widths, ext_rows, HALO)
    rolled = jnp.stack(
        [jnp.roll(states_ext, half_taps - tap_index, axis=2) for tap_index in range(TAPS)], axis=1
    )
    filtered = jnp.einsum(
        "ktqe,btelc->bkqlc", forward_matrix, rolled, preferred_element_type=jnp.float32
    ).astype(jnp.bfloat16)
    output = jnp.einsum(
        "bkqlc,kcd->bqld", filtered, mixing, preferred_element_type=jnp.float32
    ).astype(jnp.bfloat16)
    grad_ext = jnp.einsum(
        "bqld,kcd->bkqlc", cot_ext, mixing, preferred_element_type=jnp.float32
    ).astype(jnp.bfloat16)
    table_pad = jnp.pad(basis_table, ((HALO, HALO), (0, 0), (0, 0), (0, 0)))
    offset_pad = jnp.pad(offsets, ((HALO, HALO),))
    width_pad = jnp.pad(widths, ((HALO, HALO),))
    adjoint_matrix = band_matrix(
        lax.dynamic_slice_in_dim(table_pad, first_row, ext_rows, 0),
        lax.dynamic_slice_in_dim(offset_pad, first_row, ext_rows, 0),
        lax.dynamic_slice_in_dim(width_pad, first_row, ext_rows, 0),
        band_rows,
        -HALO,
    )
    grad_states = adjoint_rows(adjoint_matrix, grad_ext, half_taps).astype(jnp.bfloat16)
    grad_local = jnp.einsum(
        "bkqlc,bqld->kcd", filtered, cotangent, preferred_element_type=jnp.float32
    )
    cell_count = (
        states.shape[0] * lax.axis_size("dp") * band_rows * lax.axis_size("lat") * states.shape[2]
    )
    grad_scale = 1.0 / math.sqrt(cell_count)
    grad_mixing = lax.psum(grad_local, ("dp", "lat")) * grad_scale
    return (output, grad_states, grad_mixing)


def solution(mesh):
    in_specs = (P("dp", "lat", None, None), P(), P(), P(), P(), P("dp", "lat", None, None))
    out_specs = (P("dp", "lat", None, None), P("dp", "lat", None, None), P())
    return jax.shard_map(shards, mesh=mesh, in_specs=in_specs, out_specs=out_specs, check_vma=False)
```

profile of v0, /device:TPU:0, one launch (start us, length us, event | category | flops | bytes accessed | tf_op | source)
XLA Modules:
  0.0 218.7 jit_solution(5101938178316907386)
XLA Ops:
  7.2 0.0 copy-start
  7.2 0.0 copy-start.12
  7.2 0.0 all-reduce.5.cloned.1.call-start
  7.2 1.2 copy_bitcast_fusion
  8.4 0.2 pad_maximum_fusion
  8.6 4.3 %collective-permute-start = (bf16[2,1,4,128,128]{4,2,3,1,0:T(4,128)(2,1)S(1)}, bf16[2,1,4,128,128]{4,2,3,1,0:T(4,128)(2,1)S(1)}, u32[]{:S(2)}, u32[]{:S(2)}) collective-permute-start(bf16[2,1,4,128,128]{4,2,3,1,0:T(4,128)(2,1)S(1)} %pad_maximum_fusion), channel_id=1, source_target_pairs={{0,3},{1,4},{2,5},{3,6},{4,7},{5,8},{6,9},{7,10},{8,11},{9,12},{10... | collective-permute-start | bytes 786440 | tf_op jit(solution)/shard_map/ppermute | solution.py:15
  13.0 3.4 %collective-permute-start.1 = (bf16[2,1,4,128,128]{4,2,3,1,0:T(4,128)(2,1)S(1)}, bf16[2,1,4,128,128]{4,2,3,1,0:T(4,128)(2,1)S(1)}, u32[]{:S(2)}, u32[]{:S(2)}) collective-permute-start(bf16[2,1,4,128,128]{4,2,3,1,0:T(4,128)(2,1)S(1)} %pad_maximum_fusion), channel_id=1, source_target_pairs={{0,2},{1,3},{2,4},{3,5},{4,6},{5,7},{6,8},{7,9},{8,10},{9,11},{10,... | collective-permute-start | bytes 786440 | tf_op jit(solution)/shard_map/ppermute | solution.py:15
  16.4 2.4 %collective-permute-start.2 = (bf16[2,1,4,128,128]{4,2,3,1,0:T(4,128)(2,1)S(1)}, bf16[2,1,4,128,128]{4,2,3,1,0:T(4,128)(2,1)S(1)}, u32[]{:S(2)}, u32[]{:S(2)}) collective-permute-start(bf16[2,1,4,128,128]{4,2,3,1,0:T(4,128)(2,1)S(1)} %pad_maximum_fusion), channel_id=1, source_target_pairs={{0,1},{1,2},{2,3},{3,4},{4,5},{5,6},{6,7},{7,8},{8,9},{9,10},{10,1... | collective-permute-start | bytes 786440 | tf_op jit(solution)/shard_map/ppermute | solution.py:15
  18.8 1.3 collective-permute-start.3
  20.1 1.3 collective-permute-start.4
  21.4 0.8 pad_dynamic-slice_fusion.2
  22.2 0.1 iota_add_fusion
  22.2 0.1 iota_compare_fusion.2
  22.3 2.5 %copy.17 = bf16[64,25,9,5]{1,2,3,0:T(8,128)(2,1)S(1)} copy(bf16[64,25,9,5]{0,1,3,2:T(8,128)(2,1)} %param.7) | data formatting | bytes 288000 | tf_op args[1]
  24.8 0.7 dynamic_slice.19
  25.5 0.1 iota_compare_fusion.3
  25.6 1.2 fusion.53
  26.8 1.2 constant_dynamic-slice_fusion
  28.0 0.1 slice_bitcast_fusion.4
  28.0 0.0 collective-permute-done
  28.0 1.3 collective-permute-start.5
  29.4 0.1 dynamic-slice_add_fusion.1
  29.4 0.7 copy.21
  30.2 0.1 copy.25
  30.3 0.7 copy.19
  31.0 0.7 copy.27
  31.7 0.1 copy.23
  31.8 0.6 copy.31
  32.4 0.1 iota_add_fusion.1
  32.5 0.0 collective-permute-done.1
  32.5 0.0 collective-permute-done.2
  32.5 0.0 collective-permute-done.3
  32.5 0.0 copy-start.7
  32.6 0.9 collective-permute-done.4
  33.4 0.0 copy-done.7
  33.4 0.7 copy-done.8
  34.1 3.7 %collective-permute-done.5 = bf16[2,1,4,128,128]{4,2,3,1,0:T(4,128)(2,1)} collective-permute-done((bf16[2,1,4,128,128]{4,2,3,1,0:T(4,128)(2,1)S(1)}, bf16[2,1,4,128,128]{4,2,3,1,0:T(4,128)(2,1)}, u32[]{:S(2)}, u32[]{:S(2)}) %collective-permute-start.5) | collective-permute-done | bytes 262176 | tf_op jit(solution)/shard_map/ppermute | solution.py:15
  37.9 5.2 %concatenate.51 = bf16[2,1,28,128,128]{4,2,3,1,0:T(8,128)(2,1)S(1)} concatenate(bf16[2,1,4,128,128]{4,2,3,1,0:T(4,128)(2,1)S(1)} %collective-permute-done, bf16[2,1,4,128,128]{4,2,3,1,0:T(4,128)(2,1)S(1)} %collective-permute-done.1, bf16[2,1,4,128,128]{4,2,3,1,0:T(4,128)(2,1)S(1)} %collective-permute-done.2, bf16[2,1,4,128,128]{4,2,3,1,0:T(4,128)(2,1)S(1)} %pad_maximum_fusion, ...), dimensions={2} | concatenate | bytes 3670016 | tf_op jit(solution)/shard_map/concatenate | solution.py:53
  43.0 0.4 slice_bitcast_fusion
  43.4 0.0 copy-start.11
  43.4 2.3 %convert_bitcast_fusion = bf16[9,28,128,128]{3,2,0,1:T(8,128)(2,1)S(1)} fusion(bf16[28,128,128,1]{2,0,1,3:T(8,128)(2,1)S(1)} %get-tuple-element.6, bf16[9,128,128]{2,1,0:T(8,128)(2,1)S(1)} %copy-done), kind=kOutput, calls=%fused_computation | convolution fusion | flops 1061093376 | bytes 9469952 | tf_op jit(solution)/shard_map/bqld,kcd->bkqlc/dot_general | solution.py:91
  45.8 4.5 %fusion.20 = f32[1,4,128,128]{3,1,2,0:T(4,128)S(1)} fusion(bf16[9,28,128,128]{3,2,0,1:T(8,128)(2,1)S(1)} %convert_bitcast_fusion, bf16[9,28,4]{1,2,0:T(4,128)(2,1)S(1)} %copy-done.11), kind=kOutput, calls=%fused_computation.20 | convolution fusion | flops 33030144 | bytes 8521696 | tf_op jit(solution)/shard_map/kqe,bkqlc->belc/dot_general | solution.py:59
  50.4 4.4 %fusion.32 = f32[1,4,128,128]{3,1,2,0:T(4,128)S(1)} fusion(bf16[9,28,128,128]{3,2,0,1:T(8,128)(2,1)S(1)} %convert_bitcast_fusion, bf16[9,28,4]{1,2,0:T(4,128)(2,1)S(1)} %copy-done.10), kind=kOutput, calls=%fused_computation.24 | convolution fusion | flops 33030144 | bytes 8521696 | tf_op jit(solution)/shard_map/kqe,bkqlc->belc/dot_general | solution.py:59
  54.8 4.6 %fusion.23 = f32[1,4,128,128]{3,1,2,0:T(4,128)S(1)} fusion(bf16[9,28,128,128]{3,2,0,1:T(8,128)(2,1)S(1)} %convert_bitcast_fusion, bf16[9,28,4]{1,2,0:T(4,128)(2,1)S(1)} %copy-done.9), kind=kOutput, calls=%fused_computation.21 | convolution fusion | flops 33030144 | bytes 8521696 | tf_op jit(solution)/shard_map/kqe,bkqlc->belc/dot_general | solution.py:59
  59.4 4.4 %fusion.29 = f32[1,4,128,128]{3,1,2,0:T(4,128)S(1)} fusion(bf16[9,28,128,128]{3,2,0,1:T(8,128)(2,1)S(1)} %convert_bitcast_fusion, bf16[9,28,4]{1,2,0:T(4,128)(2,1)S(1)} %copy.25), kind=kOutput, calls=%fused_computation.23 | convolution fusion | flops 33030144 | bytes 8521696 | tf_op jit(solution)/shard_map/kqe,bkqlc->belc/dot_general | solution.py:59
  63.8 0.8 slice.127
  64.5 0.3 fusion.86
  64.9 0.3 fusion.88
  65.2 1.2 fusion.58
  66.4 1.2 fusion.59
  67.6 1.2 bitcast_dynamic-update-slice_fusion
  68.8 1.2 fusion.60
  70.0 1.2 fusion.61
  71.3 0.0 slice-start.4
  71.3 0.0 slice-start.5
  71.3 0.0 slice-start.6
  71.3 3.7 %fusion.14 = bf16[9,4,128,128]{3,0,1,2:T(8,128)(2,1)S(1)} fusion(bf16[1,5,28,128,128]{4,2,1,3,0:T(8,128)(2,1)} %fusion.61, bf16[4,25,9,5]{1,2,3,0:T(8,128)(2,1)S(1)} %copy.31, s32[4,25]{1,0:T(4,128)S(1)} %iota_add_fusion.1, pred[4,25]{1,0:T(4,128)(4,1)S(1)} %iota_compare_fusion.3), kind=kOutput, calls=%fused_computation.15 | convolution fusion | flops 166003184 | bytes 5776668 | tf_op jit(solution)/shard_map/ktqe,btelc->bkqlc/dot_general | solution.py:85
  75.0 2.5 %convolution_bitcast_fusion = f32[9,128,128]{2,1,0:T(8,128)} fusion(bf16[9,4,128,128]{3,0,1,2:T(8,128)(2,1)S(1)} %fusion.14, bf16[1,4,128,128]{3,2,1,0:T(8,128)(2,1)S(1)} %copy-done.2), kind=kOutput, calls=%fused_computation.16 | convolution fusion | flops 150994944 | bytes 1900544 | tf_op jit(solution)/shard_map/bkqlc,bqld->kcd/dot_general | solution.py:105
  77.5 0.0 all-reduce.5.cloned.1.call-update
  77.6 7.8 %fusion.50 = bf16[1,4,128,128]{3,1,2,0:T(4,128)(2,1)S(1)} fusion(bf16[9,28,128,128]{3,2,0,1:T(8,128)(2,1)} %copy-done.1, f32[1,4,2,128]{3,1,2,0:T(4,128)S(1)} %slice-done.1, f32[1,4,126,128]{3,1,2,0:T(4,128)S(1)} %slice-done, f32[1,4,1,128]{3,1,2,0:T(4,128)S(1)} %slice-done.5, f32[1,4,127,128]{3,1,2,0:T(4,128)S(1)} %slice-done.4, ...), kind=kOutput, calls=%fused_computation.31 | convolution fusion | flops 33619968 | bytes 9439200 | tf_op jit(solution)/shard_map/kqe,bkqlc->belc/dot_general | solution.py:59
  85.4 0.7 copy.29
  86.1 1.6 fusion.54
  87.6 122.3 %all-reduce.5.cloned.1.call-done = f32[9,128,128]{2,1,0:T(8,128)} async-done(((f32[9,128,128]{2,1,0:T(8,128)}), f32[9,128,128]{2,1,0:T(8,128)}) %all-reduce.5.cloned.1.call-update) | async-done | bytes 589840 | tf_op jit(solution)/shard_map/psum | solution.py:112
  210.0 1.9 broadcast_multiply_fusion
  (33 shorter events, 0.1 us)
Async XLA Ops:
  7.2 36.3 %copy-start = (bf16[9,128,128]{2,1,0:T(8,128)(2,1)S(1)}, bf16[9,128,128]{2,1,0:T(8,128)(2,1)}, u32[]{:S(2)}) copy-start(bf16[9,128,128]{2,1,0:T(8,128)(2,1)} %param.10) | copy-start | bytes 884740
  7.2 22.2 %copy-start.12 = (s32[64]{0:T(128)S(1)}, s32[64]{0:T(128)}, u32[]{:S(2)}) copy-start(s32[64]{0:T(128)} %param.8) | copy-start | bytes 772
  7.2 202.8 %all-reduce.5.cloned.1.call-start = ((), (), s32[]{:S(2)}) async-start(), calls=%async_computation | async-start | bytes 1179648 | tf_op jit(solution)/shard_map/psum | solution.py:112
  8.6 19.4 %collective-permute-start = (bf16[2,1,4,128,128]{4,2,3,1,0:T(4,128)(2,1)S(1)}, bf16[2,1,4,128,128]{4,2,3,1,0:T(4,128)(2,1)S(1)}, u32[]{:S(2)}, u32[]{:S(2)}) collective-permute-start(bf16[2,1,4,128,128]{4,2,3,1,0:T(4,128)(2,1)S(1)} %pad_maximum_fusion), channel_id=1, source_target_pairs={{0,3},{1,4},{2,5},{3,6},{4,7},{5,8},{6,9},{7,10},{8,11},{9,12},{10... | collective-permute-start | bytes 786440 | tf_op jit(solution)/shard_map/ppermute | solution.py:15
  13.0 19.5 %collective-permute-start.1 = (bf16[2,1,4,128,128]{4,2,3,1,0:T(4,128)(2,1)S(1)}, bf16[2,1,4,128,128]{4,2,3,1,0:T(4,128)(2,1)S(1)}, u32[]{:S(2)}, u32[]{:S(2)}) collective-permute-start(bf16[2,1,4,128,128]{4,2,3,1,0:T(4,128)(2,1)S(1)} %pad_maximum_fusion), channel_id=1, source_target_pairs={{0,2},{1,3},{2,4},{3,5},{4,6},{5,7},{6,8},{7,9},{8,10},{9,11},{10,... | collective-permute-start | bytes 786440 | tf_op jit(solution)/shard_map/ppermute | solution.py:15
  16.4 16.1 %collective-permute-start.2 = (bf16[2,1,4,128,128]{4,2,3,1,0:T(4,128)(2,1)S(1)}, bf16[2,1,4,128,128]{4,2,3,1,0:T(4,128)(2,1)S(1)}, u32[]{:S(2)}, u32[]{:S(2)}) collective-permute-start(bf16[2,1,4,128,128]{4,2,3,1,0:T(4,128)(2,1)S(1)} %pad_maximum_fusion), channel_id=1, source_target_pairs={{0,1},{1,2},{2,3},{3,4},{4,5},{5,6},{6,7},{7,8},{8,9},{9,10},{10,1... | collective-permute-start | bytes 786440 | tf_op jit(solution)/shard_map/ppermute | solution.py:15
  18.8 13.7 %collective-permute-start.3 = (bf16[2,1,4,128,128]{4,2,3,1,0:T(4,128)(2,1)S(1)}, bf16[2,1,4,128,128]{4,2,3,1,0:T(4,128)(2,1)S(1)}, u32[]{:S(2)}, u32[]{:S(2)}) collective-permute-start(bf16[2,1,4,128,128]{4,2,3,1,0:T(4,128)(2,1)S(1)} %pad_maximum_fusion), channel_id=1, source_target_pairs={{1,0},{2,1},{3,2},{4,3},{5,4},{6,5},{7,6},{8,7},{9,8},{10,9},{11,1... | collective-permute-start | bytes 786440 | tf_op jit(solution)/shard_map/ppermute | solution.py:15
  20.1 13.3 %collective-permute-start.4 = (bf16[2,1,4,128,128]{4,2,3,1,0:T(4,128)(2,1)S(1)}, bf16[2,1,4,128,128]{4,2,3,1,0:T(4,128)(2,1)S(1)}, u32[]{:S(2)}, u32[]{:S(2)}) collective-permute-start(bf16[2,1,4,128,128]{4,2,3,1,0:T(4,128)(2,1)S(1)} %pad_maximum_fusion), channel_id=1, source_target_pairs={{2,0},{3,1},{4,2},{5,3},{6,4},{7,5},{8,6},{9,7},{10,8},{11,9},{12,... | collective-permute-start | bytes 786440 | tf_op jit(solution)/shard_map/ppermute | solution.py:15
  28.0 9.8 %collective-permute-start.5 = (bf16[2,1,4,128,128]{4,2,3,1,0:T(4,128)(2,1)S(1)}, bf16[2,1,4,128,128]{4,2,3,1,0:T(4,128)(2,1)}, u32[]{:S(2)}, u32[]{:S(2)}) collective-permute-start(bf16[2,1,4,128,128]{4,2,3,1,0:T(4,128)(2,1)S(1)} %pad_maximum_fusion), channel_id=1, source_target_pairs={{3,0},{4,1},{5,2},{6,3},{7,4},{8,5},{9,6},{10,7},{11,8},{12,9},{13... | collective-permute-start | bytes 786440 | tf_op jit(solution)/shard_map/ppermute | solution.py:15
  32.5 0.9 copy-start.7
  33.4 0.7 copy-start.8
  43.4 2.4 %copy-start.11 = (bf16[9,28,4]{1,2,0:T(4,128)(2,1)S(1)}, bf16[9,28,4]{1,2,0:T(4,128)(2,1)}, u32[]{:S(2)}) copy-start(bf16[9,28,4]{1,2,0:T(4,128)(2,1)} %copy.19) | copy-start | bytes 6052
  45.8 13.6 %copy-start.1 = (bf16[9,28,128,128]{3,2,0,1:T(8,128)(2,1)}, bf16[9,28,128,128]{3,2,0,1:T(8,128)(2,1)S(1)}, u32[]{:S(2)}) copy-start(bf16[9,28,128,128]{3,2,0,1:T(8,128)(2,1)S(1)} %convert_bitcast_fusion) | copy-start | bytes 24772612
  45.8 4.6 %copy-start.10 = (bf16[9,28,4]{1,2,0:T(4,128)(2,1)S(1)}, bf16[9,28,4]{1,2,0:T(4,128)(2,1)}, u32[]{:S(2)}) copy-start(bf16[9,28,4]{1,2,0:T(4,128)(2,1)} %copy.27) | copy-start | bytes 6052
  50.4 4.4 %copy-start.3 = (f32[1,4,128,128]{3,1,2,0:T(4,128)}, f32[1,4,128,128]{3,1,2,0:T(4,128)S(1)}, u32[]{:S(2)}) copy-start(f32[1,4,128,128]{3,1,2,0:T(4,128)S(1)} %fusion.20) | copy-start | bytes 786436
  50.4 4.4 %copy-start.9 = (bf16[9,28,4]{1,2,0:T(4,128)(2,1)S(1)}, bf16[9,28,4]{1,2,0:T(4,128)(2,1)}, u32[]{:S(2)}) copy-start(bf16[9,28,4]{1,2,0:T(4,128)(2,1)} %copy.21) | copy-start | bytes 6052
  54.8 4.6 %copy-start.4 = (f32[1,4,128,128]{3,1,2,0:T(4,128)}, f32[1,4,128,128]{3,1,2,0:T(4,128)S(1)}, u32[]{:S(2)}) copy-start(f32[1,4,128,128]{3,1,2,0:T(4,128)S(1)} %fusion.32) | copy-start | bytes 786436
  59.4 4.4 %copy-start.5 = (f32[1,4,128,128]{3,1,2,0:T(4,128)}, f32[1,4,128,128]{3,1,2,0:T(4,128)S(1)}, u32[]{:S(2)}) copy-start(f32[1,4,128,128]{3,1,2,0:T(4,128)S(1)} %fusion.23) | copy-start | bytes 786436
  63.8 2.6 %copy-start.6 = (f32[1,4,128,128]{3,1,2,0:T(4,128)}, f32[1,4,128,128]{3,1,2,0:T(4,128)S(1)}, u32[]{:S(2)}) copy-start(f32[1,4,128,128]{3,1,2,0:T(4,128)S(1)} %fusion.29) | copy-start | bytes 786436
  70.0 4.9 %copy-start.2 = (bf16[1,4,128,128]{3,2,1,0:T(8,128)(2,1)S(1)}, bf16[1,4,128,128]{3,2,1,0:T(8,128)(2,1)}, u32[]{:S(2)}) copy-start(bf16[1,4,128,128]{3,2,1,0:T(8,128)(2,1)} %param.11) | copy-start | bytes 393220
  71.3 6.3 %slice-start = ((f32[1,4,128,128]{3,1,2,0:T(4,128)}), f32[1,4,126,128]{3,1,2,0:T(4,128)S(1)}, s32[]{:S(2)}) async-start(f32[1,4,128,128]{3,1,2,0:T(4,128)} %copy-done.3), calls=%async_computation.1 | async-start | bytes 516096 | tf_op jit(solution)/shard_map/jit(_roll_static)/slice | solution.py:65
  71.3 6.3 %slice-start.1 = ((f32[1,4,128,128]{3,1,2,0:T(4,128)}), f32[1,4,2,128]{3,1,2,0:T(4,128)S(1)}, s32[]{:S(2)}) async-start(f32[1,4,128,128]{3,1,2,0:T(4,128)} %copy-done.3), calls=%async_computation.2 | async-start | bytes 8192 | tf_op jit(solution)/shard_map/jit(_roll_static)/slice | solution.py:65
  71.3 6.3 %slice-start.2 = ((f32[1,4,128,128]{3,1,2,0:T(4,128)}), f32[1,4,126,128]{3,1,2,0:T(4,128)S(1)}, s32[]{:S(2)}) async-start(f32[1,4,128,128]{3,1,2,0:T(4,128)} %copy-done.4), calls=%async_computation.3 | async-start | bytes 516096 | tf_op jit(solution)/shard_map/jit(_roll_static)/slice | solution.py:65
  71.3 6.3 %slice-start.3 = ((f32[1,4,128,128]{3,1,2,0:T(4,128)}), f32[1,4,2,128]{3,1,2,0:T(4,128)S(1)}, s32[]{:S(2)}) async-start(f32[1,4,128,128]{3,1,2,0:T(4,128)} %copy-done.4), calls=%async_computation.4 | async-start | bytes 8192 | tf_op jit(solution)/shard_map/jit(_roll_static)/slice | solution.py:65
  71.3 6.3 %slice-start.4 = ((f32[1,4,128,128]{3,1,2,0:T(4,128)}), f32[1,4,127,128]{3,1,2,0:T(4,128)S(1)}, s32[]{:S(2)}) async-start(f32[1,4,128,128]{3,1,2,0:T(4,128)} %copy-done.5), calls=%async_computation.5 | async-start | bytes 520192 | tf_op jit(solution)/shard_map/jit(_roll_static)/slice | solution.py:65
  71.3 6.3 %slice-start.5 = ((f32[1,4,128,128]{3,1,2,0:T(4,128)}), f32[1,4,1,128]{3,1,2,0:T(4,128)S(1)}, s32[]{:S(2)}) async-start(f32[1,4,128,128]{3,1,2,0:T(4,128)} %copy-done.5), calls=%async_computation.6 | async-start | bytes 4096 | tf_op jit(solution)/shard_map/jit(_roll_static)/slice | solution.py:65
  71.3 6.3 %slice-start.6 = ((f32[1,4,128,128]{3,1,2,0:T(4,128)}), f32[1,4,1,128]{3,1,2,0:T(4,128)S(1)}, s32[]{:S(2)}) async-start(f32[1,4,128,128]{3,1,2,0:T(4,128)} %copy-done.6), calls=%async_computation.7 | async-start | bytes 4096 | tf_op jit(solution)/shard_map/jit(_roll_static)/slice | solution.py:65
Sparse Core Ops, SparseCore 0:
  77.7 132.2 all-reduce.4
where the time goes:
time: 219 us
  waiting for transfers between devices  127 us (58%)
  matrix products  37 us (17%)
  local copies, waits for them, and re-layouts  18.2 us (8%)
  between operations  14.4 us (7%)
  starting transfers between devices  14 us (6%)
  other arithmetic  8.12 us (4%)
    psum x1, waiting for transfers between devices, shards(): grad_mixing = lax.psum(grad_local, ('dp', 'lat')) * grad_scale  122 us
    dot_general x5, matrix products, adjoint_rows(): jnp.einsum('kqe,bkqlc->belc', matrix[:, tap_index], grad_filtered, prefer...  25.7 us
    ppermute x6, starting transfers between devices, shifted(): return lax.ppermute(x, axis, pairs)  14 us
    concatenate x1, local copies, waits for them, and re-layouts, halo_rows(): return jnp.concatenate(above + [stacked] + below, axis=axis_rows)  5.17 us
    unnamed x29, local copies, waits for them, and re-layouts  5.08 us
    ppermute x6, waiting for transfers between devices, shifted(): return lax.ppermute(x, axis, pairs)  4.63 us
  transfers between devices with their start and end apart: 7, of which 3 were waited for; matrix products, arithmetic and copies ran while one was open for 9% of the time, Pallas kernels for 0%

commit v1 on v0

v1 whole, which is shorter than its diff:
```python
import functools
import math

import numpy as np
import jax
import jax.numpy as jnp
from jax import lax
from jax.experimental import pallas as pl
from jax.experimental.pallas import tpu as pltpu
from jax.sharding import PartitionSpec as P

HALO = 12
LB = 4
PLANE_DP = 2
PLANE_LAT = 4
MESH = pl.DeviceIdType.MESH
BF = jnp.bfloat16
F32 = jnp.float32


def dot(a, b):
    return jnp.dot(a, b, preferred_element_type=F32)


def structure(rows, basis, taps):
    ext = rows + 2 * HALO
    hops = ext // rows
    win = LB + taps - 1
    place = np.full((8, 256), -100000, np.int32)
    for r in range(rows):
        for e in range(ext):
            p = r * ext + e
            place[0, p] = r
            place[1, p] = e - r - HALO
            place[0, 128 + p] = e - HALO
            place[1, 128 + p] = r + HALO - e
    band = basis * LB * rows
    expand = np.zeros((taps, band, basis * taps), np.float32)
    own = np.zeros((band, 256), np.float32)
    spread = np.zeros((128, hops * win * rows), np.float32)
    tap = np.zeros((taps, band, hops * win * rows), np.float32)
    for k in range(basis):
        for lp in range(LB):
            for r in range(rows):
                row = (k * LB + lp) * rows + r
                for t in range(taps):
                    expand[t, row, k * taps + t] = 1
                    for j in range(hops):
                        base = (j * win + lp + t) * rows
                        tap[t, row, base : base + rows] = 1
                own[row, r * ext : (r + 1) * ext] = 1
                own[row, 128 + r * ext : 128 + (r + 1) * ext] = 1
    for r in range(rows):
        for e in range(ext):
            for w in range(win):
                spread[r * ext + e, ((e // rows) * win + w) * rows + e % rows] = 1
    as_bf = lambda x: np.asarray(x, dtype=jnp.bfloat16)
    return place, as_bf(expand), as_bf(own), as_bf(spread), as_bf(tap)


def kernel(
    n_dp, n_lat,
    states, cot, table, offs, wids, mixing, place, expand, own, spread, tap,
    out, grad_states, grad_mix,
    buf_s, buf_c, rt, band_f, band_a, mix_t, filt, send_a, recv_a, part_b, recv_b, chunk, full,
    halo_send, halo_recv, a_send, a_recv, b_send, b_recv, d_send, d_recv,
):
    rows, lons, chans = states.shape
    basis = mixing.shape[0]
    taps = table.shape[0] // basis
    hops = buf_s.shape[0]
    reach = hops // 2
    n_plane = PLANE_DP * PLANE_LAT
    n_rest = (n_dp // PLANE_DP) * (n_lat // PLANE_LAT)
    lat_rest = n_lat // PLANE_LAT
    dp = lax.axis_index("dp")
    lat = lax.axis_index("lat")
    g = (dp % PLANE_DP) * PLANE_LAT + lat % PLANE_LAT
    z = (dp // PLANE_DP) * lat_rest + lat // PLANE_LAT

    def plane_peer(m):
        h = (g + m) % n_plane
        return h, ((dp // PLANE_DP) * PLANE_DP + h // PLANE_LAT,
                   (lat // PLANE_LAT) * PLANE_LAT + h % PLANE_LAT)

    def rest_peer(m):
        h = (z + m) % n_rest
        return h, ((h // lat_rest) * PLANE_DP + dp % PLANE_DP,
                   (h % lat_rest) * PLANE_LAT + lat % PLANE_LAT)

    dists = [d for a in range(1, reach + 1) for d in (a, -a)]

    def there(d):
        return (lat + d >= 0) & (lat + d < n_lat)

    barrier = pltpu.get_barrier_semaphore()
    for d in dists:
        @pl.when(there(d))
        def _():
            pl.semaphore_signal(barrier, inc=1, device_id=(dp, lat + d), device_id_type=MESH)
    for m in range(1, n_plane):
        pl.semaphore_signal(barrier, inc=1, device_id=plane_peer(m)[1], device_id_type=MESH)
    for m in range(1, n_rest):
        pl.semaphore_signal(barrier, inc=1, device_id=rest_peer(m)[1], device_id_type=MESH)

    half = taps // 2
    wrapped = buf_s.shape[1]
    cells = rows * lons
    r_i = lax.broadcasted_iota(jnp.int32, (wrapped, cells), 0)
    c_i = lax.broadcasted_iota(jnp.int32, (wrapped, cells), 1)
    source = (r_i % rows) * lons + (r_i // rows - half + lons) % lons
    perm = (source == c_i).astype(F32).astype(BF)
    buf_s[reach] = dot(perm, states[...].reshape(cells, chans)).astype(BF)
    buf_c[reach] = dot(perm, cot[...].reshape(cells, chans)).astype(BF)

    near = sum(there(d).astype(jnp.int32) for d in dists)
    pl.semaphore_wait(barrier, near + (n_plane - 1 + n_rest - 1))

    def halo_copy(which, buf, d):
        return pltpu.make_async_remote_copy(
            src_ref=buf.at[reach], dst_ref=buf.at[reach - d],
            send_sem=halo_send.at[which, reach + d], recv_sem=halo_recv.at[which, reach - d],
            device_id=(dp, lat + d), device_id_type=MESH)

    def halo_arrival(which, buf, d):
        return pltpu.make_async_remote_copy(
            src_ref=buf.at[reach], dst_ref=buf.at[reach + d],
            send_sem=halo_send.at[which, reach + d], recv_sem=halo_recv.at[which, reach + d],
            device_id=(dp, lat + d), device_id_type=MESH)

    for which, buf in ((0, buf_s), (1, buf_c)):
        for d in dists:
            @pl.when(there(d))
            def _():
                halo_copy(which, buf, d).start()

            @pl.when(jnp.logical_not(there(d)))
            def _():
                buf[reach + d] = jnp.zeros(buf.shape[1:], BF)

    first = lat * rows
    n_o = table.shape[2]
    support = table.shape[1]
    o_i = lax.broadcasted_iota(jnp.int32, (n_o, 256), 0)
    pick = (o_i == place[0:1, :] + first).astype(F32).astype(BF)
    both = jnp.concatenate(
        [jnp.broadcast_to(offs[...].astype(F32), (8, n_o)),
         jnp.broadcast_to(wids[...].astype(F32), (8, n_o))], axis=0).astype(BF)
    picked = dot(both, pick)
    slot = place[1:2, :].astype(F32) - picked[0:1, :]
    s_i = lax.broadcasted_iota(jnp.int32, (support, 256), 0).astype(F32)
    live = jnp.where((s_i == slot) & (s_i < picked[8:9, :]), 1.0, 0.0)
    for kt in range(basis * taps):
        rt[kt : kt + 1, :] = jnp.sum(dot(table[kt], pick) * live, axis=0, keepdims=True)
    entries = rt[...].astype(BF)
    sum_f = jnp.zeros(band_f.shape, F32)
    sum_a = jnp.zeros(band_a.shape, F32)
    for t in range(taps):
        rows_t = (dot(expand[t], entries) * own[...].astype(F32)).astype(BF)
        sum_f = sum_f + dot(rows_t[:, :128], spread[...]) * tap[t].astype(F32)
        sum_a = sum_a + dot(rows_t[:, 128:], spread[...]) * tap[taps - 1 - t].astype(F32)
    band_f[...] = sum_f.astype(BF)
    band_a[...] = sum_a.astype(BF)
    for k in range(basis):
        mix_t[k * chans : (k + 1) * chans, :] = mixing[k].astype(F32).T.astype(BF)

    step = LB * rows
    span = (LB + taps - 1) * rows
    n_blocks = lons // LB

    def filter_all(band, buf):
        for b in range(0, n_blocks, 2):
            window = jnp.concatenate(
                [jnp.concatenate([buf[j, (b + i) * step : (b + i) * step + span, :]
                                  for j in range(hops)], axis=0) for i in range(2)], axis=1)
            res = dot(band[...], window).astype(BF)
            for i in range(2):
                for k in range(basis):
                    filt[(b + i) * step : (b + i + 1) * step, k * chans : (k + 1) * chans] = (
                        res[k * step : (k + 1) * step, i * chans : (i + 1) * chans])

    u_r = lax.broadcasted_iota(jnp.int32, (cells, cells), 0)
    u_c = lax.broadcasted_iota(jnp.int32, (cells, cells), 1)
    unperm = ((u_r % lons) * rows + u_r // lons == u_c).astype(F32).astype(BF)

    def wait_halo(which, buf):
        for d in dists:
            @pl.when(there(d))
            def _():
                halo_arrival(which, buf, d).wait_recv()

    wait_halo(0, buf_s)
    filter_all(band_f, buf_s)
    mid = half * rows
    cot_rows = buf_c[reach, mid : mid + cells, :]
    grad_t = dot(cot_rows.astype(F32).T.astype(BF), filt[...])
    for k in range(basis):
        send_a[k * chans : (k + 1) * chans, :] = grad_t[:, k * chans : (k + 1) * chans].T.astype(BF)
    piece = chunk.shape[0]

    def a_copy(m):
        h, peer = plane_peer(m)
        return pltpu.make_async_remote_copy(
            src_ref=send_a.at[pl.ds(pl.multiple_of(h * piece, 16), piece)], dst_ref=recv_a.at[m],
            send_sem=a_send.at[m], recv_sem=a_recv.at[m], device_id=peer, device_id_type=MESH)

    for m in range(1, n_plane):
        a_copy(m).start()

    mixed = dot(filt[...], mixing[...].reshape(basis * chans, chans)).astype(BF)
    out[...] = dot(unperm, mixed).astype(BF).reshape(out.shape)

    wait_halo(1, buf_c)
    filter_all(band_a, buf_c)

    for m in range(1, n_plane):
        a_copy(m).wait_recv()
    total = send_a[pl.ds(pl.multiple_of(g * piece, 16), piece), :].astype(F32)
    for m in range(1, n_plane):
        total = total + recv_a[m].astype(F32)
    part_b[...] = total.astype(BF)
    recv_b[z] = total.astype(BF)

    def b_copy(m):
        return pltpu.make_async_remote_copy(
            src_ref=part_b, dst_ref=recv_b.at[z],
            send_sem=b_send.at[m], recv_sem=b_recv.at[m], device_id=rest_peer(m)[1],
            device_id_type=MESH)

    for m in range(1, n_rest):
        b_copy(m).start()

    back = dot(filt[...], mix_t[...]).astype(BF)
    grad_states[...] = dot(unperm, back).astype(BF).reshape(grad_states.shape)

    for m in range(1, n_rest):
        src = (z - m + n_rest) % n_rest
        pltpu.make_async_remote_copy(
            src_ref=part_b, dst_ref=recv_b.at[src],
            send_sem=b_send.at[m], recv_sem=b_recv.at[m], device_id=rest_peer(m)[1],
            device_id_type=MESH).wait_recv()
    total = recv_b[0].astype(F32)
    for h in range(1, n_rest):
        total = total + recv_b[h].astype(F32)
    chunk[...] = total.astype(BF)
    full[pl.ds(pl.multiple_of(g * piece, 16), piece), :] = total.astype(BF)

    def d_copy(m, owner):
        return pltpu.make_async_remote_copy(
            src_ref=chunk, dst_ref=full.at[pl.ds(pl.multiple_of(owner * piece, 16), piece)],
            send_sem=d_send.at[m], recv_sem=d_recv.at[m], device_id=plane_peer(m)[1],
            device_id_type=MESH)

    for m in range(1, n_plane):
        d_copy(m, g).start()
    for m in range(1, n_plane):
        d_copy(m, (g - m + n_plane) % n_plane).wait_recv()
    grad_mix[...] = full[...]

    for which, buf in ((0, buf_s), (1, buf_c)):
        for d in dists:
            @pl.when(there(d))
            def _():
                halo_copy(which, buf, d).wait_send()
    for m in range(1, n_plane):
        a_copy(m).wait_send()
        d_copy(m, g).wait_send()
    for m in range(1, n_rest):
        b_copy(m).wait_send()


def shards(n_dp, n_lat, states, basis_table, offsets, widths, mixing, cotangent):
    samples, rows, lons, chans = states.shape
    n_o, support, basis, taps = basis_table.shape
    hops = 1 + 2 * (HALO // rows)
    n_plane = PLANE_DP * PLANE_LAT
    n_rest = n_dp * n_lat // n_plane
    wrapped = (lons + taps - 1) * rows
    cells = rows * lons
    deep = basis * chans
    piece = deep // n_plane
    place, expand, own, spread, tap = structure(rows, basis, taps)
    table = jnp.transpose(basis_table, (2, 3, 1, 0)).reshape(basis * taps, support, n_o)
    vmem = pl.BlockSpec(memory_space=pltpu.VMEM)
    dma = pltpu.SemaphoreType.DMA
    out, grad_states, grad_mix = pl.pallas_call(
        functools.partial(kernel, n_dp, n_lat),
        out_shape=(
            jax.ShapeDtypeStruct((rows, lons, chans), BF),
            jax.ShapeDtypeStruct((rows, lons, chans), BF),
            jax.ShapeDtypeStruct((deep, chans), BF),
        ),
        in_specs=[vmem] * 11,
        out_specs=(vmem, vmem, vmem),
        scratch_shapes=[
            pltpu.VMEM((hops, wrapped, chans), BF),
            pltpu.VMEM((hops, wrapped, chans), BF),
            pltpu.VMEM((basis * taps, 256), F32),
            pltpu.VMEM(tap.shape[1:], BF),
            pltpu.VMEM(tap.shape[1:], BF),
            pltpu.VMEM((deep, chans), BF),
            pltpu.VMEM((cells, deep), BF),
            pltpu.VMEM((deep, chans), BF),
            pltpu.VMEM((n_plane, piece, chans), BF),
            pltpu.VMEM((piece, chans), BF),
            pltpu.VMEM((n_rest, piece, chans), BF),
            pltpu.VMEM((piece, chans), BF),
            pltpu.VMEM((deep, chans), BF),
            dma((2, hops)), dma((2, hops)),
            dma((n_plane,)), dma((n_plane,)),
            dma((n_rest,)), dma((n_rest,)),
            dma((n_plane,)), dma((n_plane,)),
        ],
        compiler_params=pltpu.CompilerParams(
            collective_id=0, has_side_effects=True, vmem_limit_bytes=48 * 1024 * 1024),
        cost_estimate=pl.CostEstimate(
            flops=2 * cells * deep * (3 * chans + 2 * 28 * taps),
            bytes_accessed=8 * cells * chans, transcendentals=0),
    )(states.reshape(rows, lons, chans), cotangent.reshape(rows, lons, chans), table,
      offsets.reshape(1, n_o), widths.reshape(1, n_o), mixing,
      place, expand, own, spread, tap)
    cell_count = samples * n_dp * rows * n_lat * lons
    grad_mixing = grad_mix.astype(F32).reshape(basis, chans, chans) * (1.0 / math.sqrt(cell_count))
    shape = states.shape
    return (out.reshape(shape), grad_states.reshape(shape), grad_mixing)


def solution(mesh):
    n_dp, n_lat = mesh.shape["dp"], mesh.shape["lat"]
    in_specs = (P("dp", "lat", None, None), P(), P(), P(), P(), P("dp", "lat", None, None))
    out_specs = (P("dp", "lat", None, None), P("dp", "lat", None, None), P())
    return jax.shard_map(functools.partial(shards, n_dp, n_lat), mesh=mesh, in_specs=in_specs,
                         out_specs=out_specs, check_vma=False)
```

time: 219 us -> 53.6 us (0.24)
  waiting for transfers between devices: 127 us -> 0 us
  Pallas kernels: 0 us -> 42.2 us
  matrix products: 37 us -> 0 us
  starting transfers between devices: 14 us -> 0 us
  between operations: 14.4 us -> 0.67 us
  local copies, waits for them, and re-layouts: 18.2 us -> 9.38 us
  other arithmetic: 8.12 us -> 0.86 us
    psum x1 -> x0, waiting for transfers between devices: 122 us -> none  [shards(): grad_mixing = lax.psum(grad_local, ('dp', 'lat')) * grad_scale]
    pallas_call x0 -> x1, Pallas kernels: none -> 42.2 us  [shards(): pl.pallas_call(functools.partial(kernel, n_dp, n_lat), out_shape=(jax.Sha...]
    dot_general x10 -> x0, matrix products: 37 us -> none  [the longest x5 25.7 us: adjoint_rows(): jnp.einsum('kqe,bkqlc->belc', matrix[:, tap_index], grad_filtered, prefer...]
    ppermute x6 -> x0, starting transfers between devices: 14 us -> none  [shifted(): return lax.ppermute(x, axis, pairs)]
    concatenate x1 -> x0, local copies, waits for them, and re-layouts: 5.17 us -> none  [halo_rows(): return jnp.concatenate(above + [stacked] + below, axis=axis_rows)]
    ppermute x6 -> x0, waiting for transfers between devices: 4.63 us -> none  [shifted(): return lax.ppermute(x, axis, pairs)]
    unnamed x29 -> x24, local copies, waits for them, and re-layouts: 5.08 us -> 9.38 us
    unnamed x3 -> x0, other arithmetic: 3.67 us -> none
  transfers between devices with their start and end apart: 7 -> 0, of which waited for: 3 -> 0; matrix products, arithmetic and copies ran while one was open for 9% -> 0% of each run, Pallas kernels for 0% -> 0%
where the time goes in v1:
time: 53.6 us; the launch traced here: 53.1 us
  Pallas kernels  42.2 us (79%)
  local copies, waits for them, and re-layouts  9.38 us (18%)
  other arithmetic  0.86 us (2%)
  between operations  0.67 us (1%)
    pallas_call x1, Pallas kernels, shards(): pl.pallas_call(functools.partial(kernel, n_dp, n_lat), out_shape=(jax.Sha...  42.2 us
    unnamed x24, local copies, waits for them, and re-layouts  9.38 us

profile of v1, /device:TPU:0, one launch (start us, length us, event | category | flops | bytes accessed | tf_op | source)
XLA Modules:
  0.0 53.1 jit_solution(5483570285018737136)
XLA Ops:
  0.6 0.0 copy-start.10
  0.6 0.0 copy-start.4
  0.7 0.0 copy-start.5
  0.7 0.7 %copy-done.10 = s32[8,256]{1,0:T(8,128)S(1)} copy-done((s32[8,256]{1,0:T(8,128)S(1)}, s32[8,256]{1,0:T(8,128)}, u32[]{:S(2)}) %copy-start.10) | copy-done | bytes 8216
  1.3 0.0 copy-done.4
  1.3 0.0 copy-done.5
  1.3 0.0 copy-start
  1.3 1.0 %copy-done = bf16[64,25,9,5]{0,1,3,2:T(8,128)(2,1)S(1)} copy-done((bf16[64,25,9,5]{0,1,3,2:T(8,128)(2,1)S(1)}, bf16[64,25,9,5]{0,1,3,2:T(8,128)(2,1)}, u32[]{:S(2)}) %copy-start) | copy-done | bytes 144024
  2.3 0.0 copy-start.1
  2.3 1.0 %copy-done.1 = bf16[9,128,128]{2,1,0:T(8,128)(2,1)S(1)} copy-done((bf16[9,128,128]{2,1,0:T(8,128)(2,1)S(1)}, bf16[9,128,128]{2,1,0:T(8,128)(2,1)}, u32[]{:S(2)}) %copy-start.1) | copy-done | bytes 294936
  3.3 0.0 copy-start.2
  3.3 0.9 %copy-done.2 = bf16[1,4,128,128]{3,2,1,0:T(8,128)(2,1)S(1)} copy-done((bf16[1,4,128,128]{3,2,1,0:T(8,128)(2,1)S(1)}, bf16[1,4,128,128]{3,2,1,0:T(8,128)(2,1)}, u32[]{:S(2)}) %copy-start.2) | copy-done | bytes 131096
  4.2 0.0 copy-start.3
  4.2 0.9 %copy-done.3 = bf16[1,4,128,128]{3,2,1,0:T(8,128)(2,1)S(1)} copy-done((bf16[1,4,128,128]{3,2,1,0:T(8,128)(2,1)S(1)}, bf16[1,4,128,128]{3,2,1,0:T(8,128)(2,1)}, u32[]{:S(2)}) %copy-start.3) | copy-done | bytes 131096
  5.1 0.0 copy-start.6
  5.1 1.0 %copy-done.6 = bf16[5,144,224]{2,1,0:T(8,128)(2,1)S(1)} copy-done((bf16[5,144,224]{2,1,0:T(8,128)(2,1)S(1)}, bf16[5,144,224]{2,1,0:T(8,128)(2,1)}, u32[]{:S(2)}) %copy-start.6) | copy-done | bytes 322584
  6.1 0.0 copy-start.7
  6.1 0.9 %copy-done.7 = bf16[5,144,45]{2,1,0:T(8,128)(2,1)S(1)} copy-done((bf16[5,144,45]{2,1,0:T(8,128)(2,1)S(1)}, bf16[5,144,45]{2,1,0:T(8,128)(2,1)}, u32[]{:S(2)}) %copy-start.7) | copy-done | bytes 64824
  7.0 0.0 copy-start.8
  7.0 0.9 %copy-done.8 = bf16[144,256]{1,0:T(8,128)(2,1)S(1)} copy-done((bf16[144,256]{1,0:T(8,128)(2,1)S(1)}, bf16[144,256]{1,0:T(8,128)(2,1)}, u32[]{:S(2)}) %copy-start.8) | copy-done | bytes 73752
  7.9 0.0 copy-start.9
  7.9 0.8 %copy-done.9 = bf16[128,224]{1,0:T(8,128)(2,1)S(1)} copy-done((bf16[128,224]{1,0:T(8,128)(2,1)S(1)}, bf16[128,224]{1,0:T(8,128)(2,1)}, u32[]{:S(2)}) %copy-start.9) | copy-done | bytes 57368
  8.7 42.2 %shard_map.130 = (bf16[4,128,128]{2,1,0:T(8,128)(2,1)S(1)}, bf16[4,128,128]{2,1,0:T(8,128)(2,1)S(1)}, bf16[1152,128]{1,0:T(8,128)(2,1)S(1)}) custom-call(bf16[4,128,128]{2,1,0:T(8,128)(2,1)S(1)} %bitcast.13, bf16[4,128,128]{2,1,0:T(8,128)(2,1)S(1)} %bitcast.14, bf16[45,25,64]{2,1,0:T(8,128)(2,1)S(1)} %bitcast.12, s32[1,64]{1,0:T(1,128)S(1)} %bitcast.15, ...), custom_call_target="tpu_custom_call" | custom-call | flops 783286272 | bytes 524288 | tf_op jit(solution)/shard_map/pallas_call | solution.py:286
  50.9 0.9 %convert_multiply_fusion = f32[1152,128]{1,0:T(8,128)} fusion(bf16[1152,128]{1,0:T(8,128)(2,1)S(1)} %get-tuple-element.8), kind=kLoop, calls=%fused_computation | loop fusion | flops 294912 | bytes 884736 | tf_op jit(solution)/shard_map/mul | solution.py:323
  51.8 0.7 %copy.16 = bf16[1,4,128,128]{3,2,1,0:T(8,128)(2,1)} copy(bf16[1,4,128,128]{3,2,1,0:T(8,128)(2,1)S(1)} %bitcast.11) | data formatting | bytes 262144
  52.4 0.7 %copy.17 = bf16[1,4,128,128]{3,2,1,0:T(8,128)(2,1)} copy(bf16[1,4,128,128]{3,2,1,0:T(8,128)(2,1)S(1)} %bitcast.10) | data formatting | bytes 262144
Async XLA Ops:
  0.6 0.7 %copy-start.10 = (s32[8,256]{1,0:T(8,128)S(1)}, s32[8,256]{1,0:T(8,128)}, u32[]{:S(2)}) copy-start(s32[8,256]{1,0:T(8,128)} %constant.12.clone.place) | copy-start | bytes 24580
  0.6 0.7 %copy-start.4 = (s32[64]{0:T(128)S(1)}, s32[64]{0:T(128)}, u32[]{:S(2)}) copy-start(s32[64]{0:T(128)} %param.13) | copy-start | bytes 772
  0.7 0.7 %copy-start.5 = (s32[64]{0:T(128)S(1)}, s32[64]{0:T(128)}, u32[]{:S(2)}) copy-start(s32[64]{0:T(128)} %param.14) | copy-start | bytes 772
  1.3 1.0 %copy-start = (bf16[64,25,9,5]{0,1,3,2:T(8,128)(2,1)S(1)}, bf16[64,25,9,5]{0,1,3,2:T(8,128)(2,1)}, u32[]{:S(2)}) copy-start(bf16[64,25,9,5]{0,1,3,2:T(8,128)(2,1)} %param.12) | copy-start | bytes 432004
  2.3 1.0 %copy-start.1 = (bf16[9,128,128]{2,1,0:T(8,128)(2,1)S(1)}, bf16[9,128,128]{2,1,0:T(8,128)(2,1)}, u32[]{:S(2)}) copy-start(bf16[9,128,128]{2,1,0:T(8,128)(2,1)} %mixing.1) | copy-start | bytes 884740
  3.3 0.9 %copy-start.2 = (bf16[1,4,128,128]{3,2,1,0:T(8,128)(2,1)S(1)}, bf16[1,4,128,128]{3,2,1,0:T(8,128)(2,1)}, u32[]{:S(2)}) copy-start(bf16[1,4,128,128]{3,2,1,0:T(8,128)(2,1)} %param.11) | copy-start | bytes 393220
  4.2 0.9 %copy-start.3 = (bf16[1,4,128,128]{3,2,1,0:T(8,128)(2,1)S(1)}, bf16[1,4,128,128]{3,2,1,0:T(8,128)(2,1)}, u32[]{:S(2)}) copy-start(bf16[1,4,128,128]{3,2,1,0:T(8,128)(2,1)} %param.16) | copy-start | bytes 393220
  5.1 1.0 %copy-start.6 = (bf16[5,144,224]{2,1,0:T(8,128)(2,1)S(1)}, bf16[5,144,224]{2,1,0:T(8,128)(2,1)}, u32[]{:S(2)}) copy-start(bf16[5,144,224]{2,1,0:T(8,128)(2,1)} %constant.16.clone.tap) | copy-start | bytes 967684
  6.1 0.9 %copy-start.7 = (bf16[5,144,45]{2,1,0:T(8,128)(2,1)S(1)}, bf16[5,144,45]{2,1,0:T(8,128)(2,1)}, u32[]{:S(2)}) copy-start(bf16[5,144,45]{2,1,0:T(8,128)(2,1)} %constant.13.clone.expand) | copy-start | bytes 194404
  7.0 0.9 %copy-start.8 = (bf16[144,256]{1,0:T(8,128)(2,1)S(1)}, bf16[144,256]{1,0:T(8,128)(2,1)}, u32[]{:S(2)}) copy-start(bf16[144,256]{1,0:T(8,128)(2,1)} %constant.14.clone.own) | copy-start | bytes 221188
  7.9 0.8 %copy-start.9 = (bf16[128,224]{1,0:T(8,128)(2,1)S(1)}, bf16[128,224]{1,0:T(8,128)(2,1)}, u32[]{:S(2)}) copy-start(bf16[128,224]{1,0:T(8,128)(2,1)} %constant.15.clone.spread) | copy-start | bytes 172036

commit v2 on v1

--- a/solution.py
+++ b/solution.py
@@ -60,8 +60,9 @@
 
 def kernel(
     n_dp, n_lat,
-    states, cot, table, offs, wids, mixing, place, expand, own, spread, tap,
+    states_h, cot_h, table_h, offs_h, wids_h, mixing_h, place_h, expand_h, own_h, spread_h, tap_h,
     out, grad_states, grad_mix,
+    states, cot, table, offs, wids, mixing, place, expand, own, spread, tap, load,
     buf_s, buf_c, rt, band_f, band_a, mix_t, filt, send_a, recv_a, part_b, recv_b, chunk, full,
     halo_send, halo_recv, a_send, a_recv, b_send, b_recv, d_send, d_recv,
 ):
@@ -88,13 +89,26 @@
         return h, ((h // lat_rest) * PLANE_DP + dp % PLANE_DP,
                    (h % lat_rest) * PLANE_LAT + lat % PLANE_LAT)
 
-    dists = [d for a in range(1, reach + 1) for d in (a, -a)]
+    loads = [
+        pltpu.make_async_copy(src, dst, load.at[i])
+        for i, (src, dst) in enumerate((
+            (states_h, states), (cot_h, cot), (place_h, place), (offs_h, offs), (wids_h, wids),
+            (table_h, table), (expand_h, expand), (own_h, own), (spread_h, spread),
+            (tap_h, tap), (mixing_h, mixing)))
+    ]
+    for copy in loads:
+        copy.start()
+
+    core = lat % 2
+    to_sib = 1 - 2 * core
+    third = 6 * core - 3
 
     def there(d):
         return (lat + d >= 0) & (lat + d < n_lat)
 
     barrier = pltpu.get_barrier_semaphore()
-    for d in dists:
+    pl.semaphore_signal(barrier, inc=1, device_id=(dp, lat + to_sib), device_id_type=MESH)
+    for d in (2, -2, third):
         @pl.when(there(d))
         def _():
             pl.semaphore_signal(barrier, inc=1, device_id=(dp, lat + d), device_id_type=MESH)
@@ -110,33 +124,52 @@
     c_i = lax.broadcasted_iota(jnp.int32, (wrapped, cells), 1)
     source = (r_i % rows) * lons + (r_i // rows - half + lons) % lons
     perm = (source == c_i).astype(F32).astype(BF)
+
+    def hop(which, buf, kind):
+        src, slot, d, got, sent_if, got_if = {
+            0: (reach, reach - to_sib, to_sib, reach + to_sib, None, None),
+            1: (reach, reach - 2, 2, reach - 2, there(2), there(-2)),
+            2: (reach, reach + 2, -2, reach + 2, there(-2), there(2)),
+            3: (reach, reach - third, third, reach + third, there(third), there(third)),
+            4: (reach - 2, reach - 2 - to_sib, to_sib, reach - 2 + to_sib, there(-2),
+                there(to_sib - 2)),
+            5: (reach + 2, reach + 2 - to_sib, to_sib, reach + 2 + to_sib, there(2),
+                there(to_sib + 2)),
+        }[kind]
+
+        def copy(at):
+            return pltpu.make_async_remote_copy(
+                src_ref=buf.at[src], dst_ref=buf.at[at], send_sem=halo_send.at[which, kind],
+                recv_sem=halo_recv.at[which, kind], device_id=(dp, lat + d), device_id_type=MESH)
+
+        def run(cond, f):
+            if cond is None:
+                f()
+            else:
+                pl.when(cond)(f)
+
+        return (lambda: run(sent_if, lambda: copy(slot).start()),
+                lambda: run(got_if, lambda: copy(got).wait_recv()),
+                lambda: run(sent_if, lambda: copy(slot).wait_send()))
+
+    loads[0].wait()
     buf_s[reach] = dot(perm, states[...].reshape(cells, chans)).astype(BF)
+    near = 1 + sum(there(d).astype(jnp.int32) for d in (2, -2, third))
+    pl.semaphore_wait(barrier, near + (n_plane - 1 + n_rest - 1))
+    for kind in (1, 2, 3, 0):
+        hop(0, buf_s, kind)[0]()
+    loads[1].wait()
     buf_c[reach] = dot(perm, cot[...].reshape(cells, chans)).astype(BF)
-
-    near = sum(there(d).astype(jnp.int32) for d in dists)
-    pl.semaphore_wait(barrier, near + (n_plane - 1 + n_rest - 1))
-
-    def halo_copy(which, buf, d):
-        return pltpu.make_async_remote_copy(
-            src_ref=buf.at[reach], dst_ref=buf.at[reach - d],
-            send_sem=halo_send.at[which, reach + d], recv_sem=halo_recv.at[which, reach - d],
-            device_id=(dp, lat + d), device_id_type=MESH)
-
-    def halo_arrival(which, buf, d):
-        return pltpu.make_async_remote_copy(
-            src_ref=buf.at[reach], dst_ref=buf.at[reach + d],
-            send_sem=halo_send.at[which, reach + d], recv_sem=halo_recv.at[which, reach + d],
-            device_id=(dp, lat + d), device_id_type=MESH)
-
-    for which, buf in ((0, buf_s), (1, buf_c)):
-        for d in dists:
-            @pl.when(there(d))
-            def _():
-                halo_copy(which, buf, d).start()
-
-            @pl.when(jnp.logical_not(there(d)))
-            def _():
-                buf[reach + d] = jnp.zeros(buf.shape[1:], BF)
+    for kind in (1, 2, 3, 0):
+        hop(1, buf_c, kind)[0]()
+    for buf in (buf_s, buf_c):
+        for d in range(-reach, reach + 1):
+            if d:
+                @pl.when(jnp.logical_not(there(d)))
+                def _():
+                    buf[reach + d] = jnp.zeros(buf.shape[1:], BF)
+    for copy in loads[2:]:
+        copy.wait()
 
     first = lat * rows
     n_o = table.shape[2]
@@ -183,14 +216,20 @@
     u_c = lax.broadcasted_iota(jnp.int32, (cells, cells), 1)
     unperm = ((u_r % lons) * rows + u_r // lons == u_c).astype(F32).astype(BF)
 
-    def wait_halo(which, buf):
-        for d in dists:
-            @pl.when(there(d))
-            def _():
-                halo_arrival(which, buf, d).wait_recv()
-
-    wait_halo(0, buf_s)
+    def pass_on(which, buf):
+        for kind in (1, 2):
+            hop(which, buf, kind)[1]()
+        for kind in (4, 5):
+            hop(which, buf, kind)[0]()
+
+    def wait_rest(which, buf):
+        for kind in (0, 3, 4, 5):
+            hop(which, buf, kind)[1]()
+
+    pass_on(0, buf_s)
+    wait_rest(0, buf_s)
     filter_all(band_f, buf_s)
+    pass_on(1, buf_c)
     mid = half * rows
     cot_rows = buf_c[reach, mid : mid + cells, :]
     grad_t = dot(cot_rows.astype(F32).T.astype(BF), filt[...])
@@ -210,7 +249,7 @@
     mixed = dot(filt[...], mixing[...].reshape(basis * chans, chans)).astype(BF)
     out[...] = dot(unperm, mixed).astype(BF).reshape(out.shape)
 
-    wait_halo(1, buf_c)
+    wait_rest(1, buf_c)
     filter_all(band_a, buf_c)
 
     for m in range(1, n_plane):
@@ -258,10 +297,8 @@
     grad_mix[...] = full[...]
 
     for which, buf in ((0, buf_s), (1, buf_c)):
-        for d in dists:
-            @pl.when(there(d))
-            def _():
-                halo_copy(which, buf, d).wait_send()
+        for kind in range(6):
+            hop(which, buf, kind)[2]()
     for m in range(1, n_plane):
         a_copy(m).wait_send()
         d_copy(m, g).wait_send()
@@ -281,6 +318,9 @@
     piece = deep // n_plane
     place, expand, own, spread, tap = structure(rows, basis, taps)
     table = jnp.transpose(basis_table, (2, 3, 1, 0)).reshape(basis * taps, support, n_o)
+    operands = [states.reshape(rows, lons, chans), cotangent.reshape(rows, lons, chans), table,
+                offsets.reshape(1, n_o), widths.reshape(1, n_o), mixing,
+                place, expand, own, spread, tap]
     vmem = pl.BlockSpec(memory_space=pltpu.VMEM)
     dma = pltpu.SemaphoreType.DMA
     out, grad_states, grad_mix = pl.pallas_call(
@@ -290,9 +330,10 @@
             jax.ShapeDtypeStruct((rows, lons, chans), BF),
             jax.ShapeDtypeStruct((deep, chans), BF),
         ),
-        in_specs=[vmem] * 11,
+        in_specs=[pl.BlockSpec(memory_space=pltpu.HBM)] * 11,
         out_specs=(vmem, vmem, vmem),
-        scratch_shapes=[
+        scratch_shapes=[pltpu.VMEM(x.shape, x.dtype) for x in operands] + [
+            dma((len(operands),)),
             pltpu.VMEM((hops, wrapped, chans), BF),
             pltpu.VMEM((hops, wrapped, chans), BF),
             pltpu.VMEM((basis * taps, 256), F32),
@@ -306,19 +347,17 @@
             pltpu.VMEM((n_rest, piece, chans), BF),
             pltpu.VMEM((piece, chans), BF),
             pltpu.VMEM((deep, chans), BF),
-            dma((2, hops)), dma((2, hops)),
+            dma((2, 6)), dma((2, 6)),
             dma((n_plane,)), dma((n_plane,)),
             dma((n_rest,)), dma((n_rest,)),
             dma((n_plane,)), dma((n_plane,)),
         ],
         compiler_params=pltpu.CompilerParams(
-            collective_id=0, has_side_effects=True, vmem_limit_bytes=48 * 1024 * 1024),
+            collective_id=0, has_side_effects=True, vmem_limit_bytes=63 * 1024 * 1024),
         cost_estimate=pl.CostEstimate(
             flops=2 * cells * deep * (3 * chans + 2 * 28 * taps),
             bytes_accessed=8 * cells * chans, transcendentals=0),
-    )(states.reshape(rows, lons, chans), cotangent.reshape(rows, lons, chans), table,
-      offsets.reshape(1, n_o), widths.reshape(1, n_o), mixing,
-      place, expand, own, spread, tap)
+    )(*operands)
     cell_count = samples * n_dp * rows * n_lat * lons
     grad_mixing = grad_mix.astype(F32).reshape(basis, chans, chans) * (1.0 / math.sqrt(cell_count))
     shape = states.shape

time: 53.6 us -> 39.4 us (0.74)
  local copies, waits for them, and re-layouts: 9.38 us -> 1.61 us
  Pallas kernels: 42.2 us -> 35.1 us
  other arithmetic: 0.86 us -> 1.85 us
    unnamed x24 -> x6, local copies, waits for them, and re-layouts: 9.38 us -> 1.61 us
    pallas_call x1, Pallas kernels: 42.2 us -> 35.1 us  [shards(): pl.pallas_call(functools.partial(kernel, n_dp, n_lat), out_shape=(jax.Sha...]
    mul x1, other arithmetic: 0.86 us -> 1.85 us  [shards(): grad_mix.astype(F32).reshape(basis, chans, chans)]
where the time goes in v2:
time: 39.4 us; the launch traced here: 39.2 us
  Pallas kernels  35.1 us (89%)
  other arithmetic  1.85 us (5%)
  local copies, waits for them, and re-layouts  1.61 us (4%)
  between operations  0.65 us (2%)
    pallas_call x1, Pallas kernels, shards(): pl.pallas_call(functools.partial(kernel, n_dp, n_lat), out_shape=(jax.Sha...  35.1 us
    mul x1, other arithmetic, shards(): grad_mix.astype(F32).reshape(basis, chans, chans)  1.85 us
    unnamed x6, local copies, waits for them, and re-layouts  1.61 us

profile of v2, /device:TPU:0, one launch (start us, length us, event | category | flops | bytes accessed | tf_op | source)
XLA Modules:
  0.0 39.2 jit_solution(9504428855973028248)
XLA Ops:
  0.6 35.1 %shard_map.130 = (bf16[4,128,128]{2,1,0:T(8,128)(2,1)}, bf16[4,128,128]{2,1,0:T(8,128)(2,1)}, bf16[1152,128]{1,0:T(8,128)(2,1)}) custom-call(bf16[4,128,128]{2,1,0:T(8,128)(2,1)} %bitcast.14, bf16[4,128,128]{2,1,0:T(8,128)(2,1)} %bitcast.15, bf16[45,25,64]{2,1,0:T(8,128)(2,1)} %bitcast.13, s32[1,64]{1,0:T(1,128)} %bitcast.16, s32[1,64]{1,0:T(1,128)} %bitcast.17, ...), custom_call_target="tpu_custom_call" | custom-call | flops 783286272 | bytes 524288 | tf_op jit(solution)/shard_map/pallas_call | solution.py:326
  35.8 0.0 copy-start.1
  35.8 1.9 %convert_multiply_fusion = f32[1152,128]{1,0:T(8,128)} fusion(bf16[1152,128]{1,0:T(8,128)(2,1)} %get-tuple-element.8), kind=kLoop, calls=%fused_computation | loop fusion | flops 294912 | bytes 884736 | tf_op jit(solution)/shard_map/mul | solution.py:362
  37.6 0.0 copy-done.1
  37.6 0.0 copy-start
  37.6 0.7 %copy.16 = bf16[1,4,128,128]{3,2,1,0:T(8,128)(2,1)} copy(bf16[1,4,128,128]{3,2,1,0:T(8,128)(2,1)S(1)} %bitcast.12) | data formatting | bytes 262144
  38.3 0.3 copy-done
  38.6 0.7 %copy.17 = bf16[1,4,128,128]{3,2,1,0:T(8,128)(2,1)} copy(bf16[1,4,128,128]{3,2,1,0:T(8,128)(2,1)S(1)} %bitcast.11) | data formatting | bytes 262144
Async XLA Ops:
  35.8 1.9 %copy-start.1 = (bf16[4,128,128]{2,1,0:T(8,128)(2,1)S(1)}, bf16[4,128,128]{2,1,0:T(8,128)(2,1)}, u32[]{:S(2)}) copy-start(bf16[4,128,128]{2,1,0:T(8,128)(2,1)} %get-tuple-element.6) | copy-start | bytes 393220
  37.6 1.0 %copy-start = (bf16[4,128,128]{2,1,0:T(8,128)(2,1)S(1)}, bf16[4,128,128]{2,1,0:T(8,128)(2,1)}, u32[]{:S(2)}) copy-start(bf16[4,128,128]{2,1,0:T(8,128)(2,1)} %get-tuple-element.7) | copy-start | bytes 393220

commit v3 on v2

--- a/solution.py
+++ b/solution.py
@@ -61,7 +61,8 @@
 def kernel(
     n_dp, n_lat,
     states_h, cot_h, table_h, offs_h, wids_h, mixing_h, place_h, expand_h, own_h, spread_h, tap_h,
-    out, grad_states, grad_mix,
+    out_h, grad_states_h, grad_mix_h,
+    out, grad_states, store,
     states, cot, table, offs, wids, mixing, place, expand, own, spread, tap, load,
     buf_s, buf_c, rt, band_f, band_a, mix_t, filt, send_a, recv_a, part_b, recv_b, chunk, full,
     halo_send, halo_recv, a_send, a_recv, b_send, b_recv, d_send, d_recv,
@@ -120,9 +121,12 @@
     half = taps // 2
     wrapped = buf_s.shape[1]
     cells = rows * lons
+    rows_log, lons_log = rows.bit_length() - 1, lons.bit_length() - 1
     r_i = lax.broadcasted_iota(jnp.int32, (wrapped, cells), 0)
     c_i = lax.broadcasted_iota(jnp.int32, (wrapped, cells), 1)
-    source = (r_i % rows) * lons + (r_i // rows - half + lons) % lons
+    turned = jnp.where(r_i >= half * rows, r_i - half * rows, r_i + cells - half * rows)
+    turned = jnp.where(turned >= cells, turned - cells, turned)
+    source = (turned & (rows - 1)) * lons + (turned >> rows_log)
     perm = (source == c_i).astype(F32).astype(BF)
 
     def hop(which, buf, kind):
@@ -160,8 +164,6 @@
         hop(0, buf_s, kind)[0]()
     loads[1].wait()
     buf_c[reach] = dot(perm, cot[...].reshape(cells, chans)).astype(BF)
-    for kind in (1, 2, 3, 0):
-        hop(1, buf_c, kind)[0]()
     for buf in (buf_s, buf_c):
         for d in range(-reach, reach + 1):
             if d:
@@ -186,16 +188,15 @@
     for kt in range(basis * taps):
         rt[kt : kt + 1, :] = jnp.sum(dot(table[kt], pick) * live, axis=0, keepdims=True)
     entries = rt[...].astype(BF)
-    sum_f = jnp.zeros(band_f.shape, F32)
-    sum_a = jnp.zeros(band_a.shape, F32)
-    for t in range(taps):
-        rows_t = (dot(expand[t], entries) * own[...].astype(F32)).astype(BF)
-        sum_f = sum_f + dot(rows_t[:, :128], spread[...]) * tap[t].astype(F32)
-        sum_a = sum_a + dot(rows_t[:, 128:], spread[...]) * tap[taps - 1 - t].astype(F32)
-    band_f[...] = sum_f.astype(BF)
-    band_a[...] = sum_a.astype(BF)
-    for k in range(basis):
-        mix_t[k * chans : (k + 1) * chans, :] = mixing[k].astype(F32).T.astype(BF)
+
+    def build(band, lanes, tap_of):
+        acc = jnp.zeros(band.shape, F32)
+        for t in range(taps):
+            rows_t = (dot(expand[t], entries[:, lanes]) * own[:, lanes].astype(F32)).astype(BF)
+            acc = acc + dot(rows_t, spread[...]) * tap[tap_of(t)].astype(F32)
+        band[...] = acc.astype(BF)
+
+    build(band_f, slice(0, 128), lambda t: t)
 
     step = LB * rows
     span = (LB + taps - 1) * rows
@@ -214,7 +215,7 @@
 
     u_r = lax.broadcasted_iota(jnp.int32, (cells, cells), 0)
     u_c = lax.broadcasted_iota(jnp.int32, (cells, cells), 1)
-    unperm = ((u_r % lons) * rows + u_r // lons == u_c).astype(F32).astype(BF)
+    unperm = ((u_r & (lons - 1)) * rows + (u_r >> lons_log) == u_c).astype(F32).astype(BF)
 
     def pass_on(which, buf):
         for kind in (1, 2):
@@ -226,10 +227,17 @@
         for kind in (0, 3, 4, 5):
             hop(which, buf, kind)[1]()
 
+    def unpermuted(x, ref):
+        ref[...] = dot(unperm, x.astype(BF)).astype(BF).reshape(ref.shape)
+
+    stores = [pltpu.make_async_copy(src, dst, store.at[i]) for i, (src, dst) in enumerate(
+        ((out, out_h), (grad_states, grad_states_h), (full, grad_mix_h)))]
+
     pass_on(0, buf_s)
+    for kind in (1, 2, 3, 0):
+        hop(1, buf_c, kind)[0]()
     wait_rest(0, buf_s)
     filter_all(band_f, buf_s)
-    pass_on(1, buf_c)
     mid = half * rows
     cot_rows = buf_c[reach, mid : mid + cells, :]
     grad_t = dot(cot_rows.astype(F32).T.astype(BF), filt[...])
@@ -246,11 +254,12 @@
     for m in range(1, n_plane):
         a_copy(m).start()
 
-    mixed = dot(filt[...], mixing[...].reshape(basis * chans, chans)).astype(BF)
-    out[...] = dot(unperm, mixed).astype(BF).reshape(out.shape)
-
-    wait_rest(1, buf_c)
-    filter_all(band_a, buf_c)
+    pass_on(1, buf_c)
+    unpermuted(dot(filt[...], mixing[...].reshape(basis * chans, chans)), out)
+    stores[0].start()
+    build(band_a, slice(128, 256), lambda t: taps - 1 - t)
+    for k in range(basis):
+        mix_t[k * chans : (k + 1) * chans, :] = mixing[k].astype(F32).T.astype(BF)
 
     for m in range(1, n_plane):
         a_copy(m).wait_recv()
@@ -260,24 +269,20 @@
     part_b[...] = total.astype(BF)
     recv_b[z] = total.astype(BF)
 
-    def b_copy(m):
+    def b_copy(m, owner):
         return pltpu.make_async_remote_copy(
-            src_ref=part_b, dst_ref=recv_b.at[z],
+            src_ref=part_b, dst_ref=recv_b.at[owner],
             send_sem=b_send.at[m], recv_sem=b_recv.at[m], device_id=rest_peer(m)[1],
             device_id_type=MESH)
 
     for m in range(1, n_rest):
-        b_copy(m).start()
-
-    back = dot(filt[...], mix_t[...]).astype(BF)
-    grad_states[...] = dot(unperm, back).astype(BF).reshape(grad_states.shape)
+        b_copy(m, z).start()
+
+    wait_rest(1, buf_c)
+    filter_all(band_a, buf_c)
 
     for m in range(1, n_rest):
-        src = (z - m + n_rest) % n_rest
-        pltpu.make_async_remote_copy(
-            src_ref=part_b, dst_ref=recv_b.at[src],
-            send_sem=b_send.at[m], recv_sem=b_recv.at[m], device_id=rest_peer(m)[1],
-            device_id_type=MESH).wait_recv()
+        b_copy(m, (z - m + n_rest) % n_rest).wait_recv()
     total = recv_b[0].astype(F32)
     for h in range(1, n_rest):
         total = total + recv_b[h].astype(F32)
@@ -292,9 +297,13 @@
 
     for m in range(1, n_plane):
         d_copy(m, g).start()
+
+    unpermuted(dot(filt[...], mix_t[...]), grad_states)
+    stores[1].start()
+
     for m in range(1, n_plane):
         d_copy(m, (g - m + n_plane) % n_plane).wait_recv()
-    grad_mix[...] = full[...]
+    stores[2].start()
 
     for which, buf in ((0, buf_s), (1, buf_c)):
         for kind in range(6):
@@ -303,7 +312,25 @@
         a_copy(m).wait_send()
         d_copy(m, g).wait_send()
     for m in range(1, n_rest):
-        b_copy(m).wait_send()
+        b_copy(m, z).wait_send()
+    for copy in stores:
+        copy.wait()
+
+
+def finish(scale, out_in, grad_in, mix_in, out, grad_states, grad_mix, held, wide, sems):
+    read = pltpu.make_async_copy(mix_in, held, sems.at[0])
+    read.start()
+    first = pltpu.make_async_copy(out_in, out, sems.at[1])
+    second = pltpu.make_async_copy(grad_in, grad_states, sems.at[2])
+    first.start()
+    second.start()
+    read.wait()
+    wide[...] = held[...].astype(F32) * scale
+    write = pltpu.make_async_copy(wide, grad_mix, sems.at[3])
+    write.start()
+    first.wait()
+    second.wait()
+    write.wait()
 
 
 def shards(n_dp, n_lat, states, basis_table, offsets, widths, mixing, cotangent):
@@ -321,7 +348,7 @@
     operands = [states.reshape(rows, lons, chans), cotangent.reshape(rows, lons, chans), table,
                 offsets.reshape(1, n_o), widths.reshape(1, n_o), mixing,
                 place, expand, own, spread, tap]
-    vmem = pl.BlockSpec(memory_space=pltpu.VMEM)
+    hbm = pl.BlockSpec(memory_space=pltpu.HBM)
     dma = pltpu.SemaphoreType.DMA
     out, grad_states, grad_mix = pl.pallas_call(
         functools.partial(kernel, n_dp, n_lat),
@@ -330,9 +357,9 @@
             jax.ShapeDtypeStruct((rows, lons, chans), BF),
             jax.ShapeDtypeStruct((deep, chans), BF),
         ),
-        in_specs=[pl.BlockSpec(memory_space=pltpu.HBM)] * 11,
-        out_specs=(vmem, vmem, vmem),
-        scratch_shapes=[pltpu.VMEM(x.shape, x.dtype) for x in operands] + [
+        in_specs=[hbm] * 11,
+        out_specs=(hbm, hbm, hbm),
+        scratch_shapes=[pltpu.VMEM((rows, lons, chans), BF)] * 2 + [dma((3,))] + [pltpu.VMEM(x.shape, x.dtype) for x in operands] + [
             dma((len(operands),)),
             pltpu.VMEM((hops, wrapped, chans), BF),
             pltpu.VMEM((hops, wrapped, chans), BF),
@@ -359,9 +386,23 @@
             bytes_accessed=8 * cells * chans, transcendentals=0),
     )(*operands)
     cell_count = samples * n_dp * rows * n_lat * lons
-    grad_mixing = grad_mix.astype(F32).reshape(basis, chans, chans) * (1.0 / math.sqrt(cell_count))
+    scale = 1.0 / math.sqrt(cell_count)
+    out, grad_states, grad_mixing = pl.pallas_call(
+        functools.partial(finish, scale),
+        out_shape=(
+            jax.ShapeDtypeStruct((rows, lons, chans), BF),
+            jax.ShapeDtypeStruct((rows, lons, chans), BF),
+            jax.ShapeDtypeStruct((deep, chans), F32),
+        ),
+        in_specs=[hbm] * 3,
+        out_specs=(hbm, hbm, hbm),
+        scratch_shapes=[pltpu.VMEM((deep, chans), BF), pltpu.VMEM((deep, chans), F32),
+                        dma((4,))],
+        compiler_params=pltpu.CompilerParams(vmem_limit_bytes=63 * 1024 * 1024),
+    )(out, grad_states, grad_mix)
     shape = states.shape
-    return (out.reshape(shape), grad_states.reshape(shape), grad_mixing)
+    return (out.reshape(shape), grad_states.reshape(shape),
+            grad_mixing.reshape(basis, chans, chans))
 
 
 def solution(mesh):

time: 39.4 us -> 42 us (1.066)
  Pallas kernels: 35.1 us -> 41.2 us
  other arithmetic: 1.85 us -> 0 us
  local copies, waits for them, and re-layouts: 1.61 us -> 0 us
    pallas_call x0 -> x1, Pallas kernels: none -> 9.08 us  [shards(): pl.pallas_call(functools.partial(finish, scale), out_shape=(jax.ShapeDtyp...]
    pallas_call x1, Pallas kernels: 35.1 us -> 32.2 us  [shards(): pl.pallas_call(functools.partial(kernel, n_dp, n_lat), out_shape=(jax.Sha...]
    mul x1 -> x0, other arithmetic: 1.85 us -> none  [shards(): grad_mix.astype(F32).reshape(basis, chans, chans)]
    unnamed x6 -> x0, local copies, waits for them, and re-layouts: 1.61 us -> none
where the time goes in v3:
time: 42 us; the launch traced here: 41.9 us
  Pallas kernels  41.2 us (98%)
  between operations  0.64 us (2%)
    pallas_call x1, Pallas kernels, shards(): pl.pallas_call(functools.partial(kernel, n_dp, n_lat), out_shape=(jax.Sha...  32.2 us
    pallas_call x1, Pallas kernels, shards(): pl.pallas_call(functools.partial(finish, scale), out_shape=(jax.ShapeDtyp...  9.08 us

profile of v3, /device:TPU:0, one launch (start us, length us, event | category | flops | bytes accessed | tf_op | source)
XLA Modules:
  0.0 41.9 jit_solution(8854782037921925917)
XLA Ops:
  0.6 32.2 %shard_map.130 = (bf16[4,128,128]{2,1,0:T(8,128)(2,1)}, bf16[4,128,128]{2,1,0:T(8,128)(2,1)}, bf16[1152,128]{1,0:T(8,128)(2,1)}) custom-call(bf16[4,128,128]{2,1,0:T(8,128)(2,1)} %bitcast.12, bf16[4,128,128]{2,1,0:T(8,128)(2,1)} %bitcast.13, bf16[45,25,64]{2,1,0:T(8,128)(2,1)} %bitcast.11, s32[1,64]{1,0:T(1,128)} %bitcast.16, s32[1,64]{1,0:T(1,128)} %bitcast.17, ...), custom_call_target="tpu_custom_call" | custom-call | flops 783286272 | bytes 524288 | tf_op jit(solution)/shard_map/pallas_call | solution.py:353
  32.8 9.1 %shard_map.131 = (bf16[4,128,128]{2,1,0:T(8,128)(2,1)}, bf16[4,128,128]{2,1,0:T(8,128)(2,1)}, f32[1152,128]{1,0:T(8,128)}) custom-call(bf16[4,128,128]{2,1,0:T(8,128)(2,1)} %get-tuple-element.9.out_in, bf16[4,128,128]{2,1,0:T(8,128)(2,1)} %get-tuple-element.10.grad_in, bf16[1152,128]{1,0:T(8,128)(2,1)} %get-tuple-element.11.mix_in), custom_call_target="tpu_custom_call" | custom-call | tf_op jit(solution)/shard_map/pallas_call | solution.py:390

commit v4 on v3

--- a/solution.py
+++ b/solution.py
@@ -13,6 +13,7 @@
 LB = 4
 PLANE_DP = 2
 PLANE_LAT = 4
+PARTS = 3
 MESH = pl.DeviceIdType.MESH
 BF = jnp.bfloat16
 F32 = jnp.float32
@@ -244,15 +245,21 @@
     for k in range(basis):
         send_a[k * chans : (k + 1) * chans, :] = grad_t[:, k * chans : (k + 1) * chans].T.astype(BF)
     piece = chunk.shape[0]
-
-    def a_copy(m):
+    cut = piece // PARTS
+
+    def rows_of(owner, i):
+        return pl.ds(pl.multiple_of(owner * piece + i * cut, 16), cut)
+
+    def a_copy(m, i):
         h, peer = plane_peer(m)
         return pltpu.make_async_remote_copy(
-            src_ref=send_a.at[pl.ds(pl.multiple_of(h * piece, 16), piece)], dst_ref=recv_a.at[m],
-            send_sem=a_send.at[m], recv_sem=a_recv.at[m], device_id=peer, device_id_type=MESH)
-
-    for m in range(1, n_plane):
-        a_copy(m).start()
+            src_ref=send_a.at[rows_of(h, i)], dst_ref=recv_a.at[m, pl.ds(i * cut, cut)],
+            send_sem=a_send.at[m, i], recv_sem=a_recv.at[m, i], device_id=peer,
+            device_id_type=MESH)
+
+    for i in range(PARTS):
+        for m in range(1, n_plane):
+            a_copy(m, i).start()
 
     pass_on(1, buf_c)
     unpermuted(dot(filt[...], mixing[...].reshape(basis * chans, chans)), out)
@@ -261,76 +268,87 @@
     for k in range(basis):
         mix_t[k * chans : (k + 1) * chans, :] = mixing[k].astype(F32).T.astype(BF)
 
-    for m in range(1, n_plane):
-        a_copy(m).wait_recv()
-    total = send_a[pl.ds(pl.multiple_of(g * piece, 16), piece), :].astype(F32)
-    for m in range(1, n_plane):
-        total = total + recv_a[m].astype(F32)
-    part_b[...] = total.astype(BF)
-    recv_b[z] = total.astype(BF)
-
-    def b_copy(m, owner):
+    def b_copy(m, owner, i):
         return pltpu.make_async_remote_copy(
-            src_ref=part_b, dst_ref=recv_b.at[owner],
-            send_sem=b_send.at[m], recv_sem=b_recv.at[m], device_id=rest_peer(m)[1],
+            src_ref=part_b.at[pl.ds(i * cut, cut)], dst_ref=recv_b.at[owner, pl.ds(i * cut, cut)],
+            send_sem=b_send.at[m, i], recv_sem=b_recv.at[m, i], device_id=rest_peer(m)[1],
             device_id_type=MESH)
 
-    for m in range(1, n_rest):
-        b_copy(m, z).start()
+    for i in range(PARTS):
+        at = slice(i * cut, (i + 1) * cut)
+        total = send_a[rows_of(g, i), :].astype(F32)
+        for m in range(1, n_plane):
+            a_copy(m, i).wait_recv()
+        for m in range(1, n_plane):
+            total = total + recv_a[m, at, :].astype(F32)
+        part_b[at, :] = total.astype(BF)
+        recv_b[z, at, :] = total.astype(BF)
+        for m in range(1, n_rest):
+            b_copy(m, z, i).start()
 
     wait_rest(1, buf_c)
     filter_all(band_a, buf_c)
 
-    for m in range(1, n_rest):
-        b_copy(m, (z - m + n_rest) % n_rest).wait_recv()
-    total = recv_b[0].astype(F32)
-    for h in range(1, n_rest):
-        total = total + recv_b[h].astype(F32)
-    chunk[...] = total.astype(BF)
-    full[pl.ds(pl.multiple_of(g * piece, 16), piece), :] = total.astype(BF)
-
-    def d_copy(m, owner):
+    def d_copy(m, owner, i):
         return pltpu.make_async_remote_copy(
-            src_ref=chunk, dst_ref=full.at[pl.ds(pl.multiple_of(owner * piece, 16), piece)],
-            send_sem=d_send.at[m], recv_sem=d_recv.at[m], device_id=plane_peer(m)[1],
+            src_ref=chunk.at[pl.ds(i * cut, cut)], dst_ref=full.at[rows_of(owner, i)],
+            send_sem=d_send.at[m, i], recv_sem=d_recv.at[m, i], device_id=plane_peer(m)[1],
             device_id_type=MESH)
 
-    for m in range(1, n_plane):
-        d_copy(m, g).start()
+    for i in range(PARTS):
+        at = slice(i * cut, (i + 1) * cut)
+        for m in range(1, n_rest):
+            b_copy(m, (z - m + n_rest) % n_rest, i).wait_recv()
+        total = recv_b[0, at, :].astype(F32)
+        for h in range(1, n_rest):
+            total = total + recv_b[h, at, :].astype(F32)
+        chunk[at, :] = total.astype(BF)
+        full[rows_of(g, i), :] = total.astype(BF)
+        for m in range(1, n_plane):
+            d_copy(m, g, i).start()
 
     unpermuted(dot(filt[...], mix_t[...]), grad_states)
     stores[1].start()
 
-    for m in range(1, n_plane):
-        d_copy(m, (g - m + n_plane) % n_plane).wait_recv()
+    for i in range(PARTS):
+        for m in range(1, n_plane):
+            d_copy(m, (g - m + n_plane) % n_plane, i).wait_recv()
     stores[2].start()
 
     for which, buf in ((0, buf_s), (1, buf_c)):
         for kind in range(6):
             hop(which, buf, kind)[2]()
-    for m in range(1, n_plane):
-        a_copy(m).wait_send()
-        d_copy(m, g).wait_send()
-    for m in range(1, n_rest):
-        b_copy(m, z).wait_send()
+    for i in range(PARTS):
+        for m in range(1, n_plane):
+            a_copy(m, i).wait_send()
+            d_copy(m, g, i).wait_send()
+        for m in range(1, n_rest):
+            b_copy(m, z, i).wait_send()
     for copy in stores:
         copy.wait()
 
 
-def finish(scale, out_in, grad_in, mix_in, out, grad_states, grad_mix, held, wide, sems):
-    read = pltpu.make_async_copy(mix_in, held, sems.at[0])
-    read.start()
-    first = pltpu.make_async_copy(out_in, out, sems.at[1])
-    second = pltpu.make_async_copy(grad_in, grad_states, sems.at[2])
-    first.start()
-    second.start()
-    read.wait()
-    wide[...] = held[...].astype(F32) * scale
-    write = pltpu.make_async_copy(wide, grad_mix, sems.at[3])
-    write.start()
-    first.wait()
-    second.wait()
-    write.wait()
+def finish(scale, out_in, grad_in, mix_in, out, grad_states, grad_mix, first, second, held, wide,
+           sems):
+    deep = held.shape[0]
+    cut = deep // PARTS
+    reads, writes = [], []
+    for i in range(PARTS):
+        rows = pl.ds(i * cut, cut)
+        reads.append(pltpu.make_async_copy(mix_in.at[rows], held.at[rows], sems.at[0, i]))
+        writes.append(pltpu.make_async_copy(wide.at[rows], grad_mix.at[rows], sems.at[1, i]))
+    for i, (src, via, dst) in enumerate(((out_in, first, out), (grad_in, second, grad_states))):
+        reads.append(pltpu.make_async_copy(src, via, sems.at[0, PARTS + i]))
+        writes.append(pltpu.make_async_copy(via, dst, sems.at[1, PARTS + i]))
+    for copy in reads:
+        copy.start()
+    for i in range(PARTS + 2):
+        reads[i].wait()
+        if i < PARTS:
+            wide[i * cut : (i + 1) * cut, :] = held[i * cut : (i + 1) * cut, :].astype(F32) * scale
+        writes[i].start()
+    for copy in writes:
+        copy.wait()
 
 
 def shards(n_dp, n_lat, states, basis_table, offsets, widths, mixing, cotangent):
@@ -375,9 +393,9 @@
             pltpu.VMEM((piece, chans), BF),
             pltpu.VMEM((deep, chans), BF),
             dma((2, 6)), dma((2, 6)),
-            dma((n_plane,)), dma((n_plane,)),
-            dma((n_rest,)), dma((n_rest,)),
-            dma((n_plane,)), dma((n_plane,)),
+            dma((n_plane, PARTS)), dma((n_plane, PARTS)),
+            dma((n_rest, PARTS)), dma((n_rest, PARTS)),
+            dma((n_plane, PARTS)), dma((n_plane, PARTS)),
         ],
         compiler_params=pltpu.CompilerParams(
             collective_id=0, has_side_effects=True, vmem_limit_bytes=63 * 1024 * 1024),
@@ -396,8 +414,8 @@
         ),
         in_specs=[hbm] * 3,
         out_specs=(hbm, hbm, hbm),
-        scratch_shapes=[pltpu.VMEM((deep, chans), BF), pltpu.VMEM((deep, chans), F32),
-                        dma((4,))],
+        scratch_shapes=[pltpu.VMEM((rows, lons, chans), BF)] * 2 + [
+            pltpu.VMEM((deep, chans), BF), pltpu.VMEM((deep, chans), F32), dma((2, PARTS + 2))],
         compiler_params=pltpu.CompilerParams(vmem_limit_bytes=63 * 1024 * 1024),
     )(out, grad_states, grad_mix)
     shape = states.shape

time: 42 us -> 35.9 us (0.85)
  Pallas kernels: 41.2 us -> 35.1 us
    pallas_call x1, Pallas kernels: 9.08 us -> 1.89 us  [shards(): pl.pallas_call(functools.partial(finish, scale), out_shape=(jax.ShapeDtyp...]
    pallas_call x1, Pallas kernels: 32.2 us -> 33.2 us  [shards(): pl.pallas_call(functools.partial(kernel, n_dp, n_lat), out_shape=(jax.Sha...]
where the time goes in v4:
time: 35.9 us; the launch traced here: 35.8 us
  Pallas kernels  35.1 us (98%)
  between operations  0.64 us (2%)
    pallas_call x1, Pallas kernels, shards(): pl.pallas_call(functools.partial(kernel, n_dp, n_lat), out_shape=(jax.Sha...  33.2 us
    pallas_call x1, Pallas kernels, shards(): pl.pallas_call(functools.partial(finish, scale), out_shape=(jax.ShapeDtyp...  1.89 us

profile of v4, /device:TPU:0, one launch (start us, length us, event | category | flops | bytes accessed | tf_op | source)
XLA Modules:
  0.0 35.8 jit_solution(9671542815538813249)
XLA Ops:
  0.6 33.2 %shard_map.130 = (bf16[4,128,128]{2,1,0:T(8,128)(2,1)}, bf16[4,128,128]{2,1,0:T(8,128)(2,1)}, bf16[1152,128]{1,0:T(8,128)(2,1)}) custom-call(bf16[4,128,128]{2,1,0:T(8,128)(2,1)} %bitcast.12, bf16[4,128,128]{2,1,0:T(8,128)(2,1)} %bitcast.13, bf16[45,25,64]{2,1,0:T(8,128)(2,1)} %bitcast.11, s32[1,64]{1,0:T(1,128)} %bitcast.16, s32[1,64]{1,0:T(1,128)} %bitcast.17, ...), custom_call_target="tpu_custom_call" | custom-call | flops 783286272 | bytes 524288 | tf_op jit(solution)/shard_map/pallas_call | solution.py:371
  33.9 1.9 %shard_map.131 = (bf16[4,128,128]{2,1,0:T(8,128)(2,1)}, bf16[4,128,128]{2,1,0:T(8,128)(2,1)}, f32[1152,128]{1,0:T(8,128)}) custom-call(bf16[4,128,128]{2,1,0:T(8,128)(2,1)} %get-tuple-element.9.out_in, bf16[4,128,128]{2,1,0:T(8,128)(2,1)} %get-tuple-element.10.grad_in, bf16[1152,128]{1,0:T(8,128)(2,1)} %get-tuple-element.11.mix_in), custom_call_target="tpu_custom_call" | custom-call | tf_op jit(solution)/shard_map/pallas_call | solution.py:408

commit v5 on v4

--- a/solution.py
+++ b/solution.py
@@ -13,7 +13,8 @@
 LB = 4
 PLANE_DP = 2
 PLANE_LAT = 4
-PARTS = 3
+PARTS = 1
+WRITES = 3
 MESH = pl.DeviceIdType.MESH
 BF = jnp.bfloat16
 F32 = jnp.float32
@@ -63,7 +64,7 @@
     n_dp, n_lat,
     states_h, cot_h, table_h, offs_h, wids_h, mixing_h, place_h, expand_h, own_h, spread_h, tap_h,
     out_h, grad_states_h, grad_mix_h,
-    out, grad_states, store,
+    out, grad_states, cot_t, store,
     states, cot, table, offs, wids, mixing, place, expand, own, spread, tap, load,
     buf_s, buf_c, rt, band_f, band_a, mix_t, filt, send_a, recv_a, part_b, recv_b, chunk, full,
     halo_send, halo_recv, a_send, a_recv, b_send, b_recv, d_send, d_recv,
@@ -130,7 +131,10 @@
     source = (turned & (rows - 1)) * lons + (turned >> rows_log)
     perm = (source == c_i).astype(F32).astype(BF)
 
-    def hop(which, buf, kind):
+    head = (lons // 2 + taps - 1) * rows
+    halves = (((0, head), (head, wrapped - head)), ((0, wrapped),))
+
+    def hop(which, buf, kind, part):
         src, slot, d, got, sent_if, got_if = {
             0: (reach, reach - to_sib, to_sib, reach + to_sib, None, None),
             1: (reach, reach - 2, 2, reach - 2, there(2), there(-2)),
@@ -142,10 +146,13 @@
                 there(to_sib + 2)),
         }[kind]
 
+        span_of = pl.ds(*halves[which][part])
+
         def copy(at):
             return pltpu.make_async_remote_copy(
-                src_ref=buf.at[src], dst_ref=buf.at[at], send_sem=halo_send.at[which, kind],
-                recv_sem=halo_recv.at[which, kind], device_id=(dp, lat + d), device_id_type=MESH)
+                src_ref=buf.at[src, span_of], dst_ref=buf.at[at, span_of],
+                send_sem=halo_send.at[which, kind, part], recv_sem=halo_recv.at[which, kind, part],
+                device_id=(dp, lat + d), device_id_type=MESH)
 
         def run(cond, f):
             if cond is None:
@@ -161,8 +168,9 @@
     buf_s[reach] = dot(perm, states[...].reshape(cells, chans)).astype(BF)
     near = 1 + sum(there(d).astype(jnp.int32) for d in (2, -2, third))
     pl.semaphore_wait(barrier, near + (n_plane - 1 + n_rest - 1))
-    for kind in (1, 2, 3, 0):
-        hop(0, buf_s, kind)[0]()
+    for part in range(2):
+        for kind in (1, 2, 3, 0):
+            hop(0, buf_s, kind, part)[0]()
     loads[1].wait()
     buf_c[reach] = dot(perm, cot[...].reshape(cells, chans)).astype(BF)
     for buf in (buf_s, buf_c):
@@ -198,13 +206,18 @@
         band[...] = acc.astype(BF)
 
     build(band_f, slice(0, 128), lambda t: t)
+    build(band_a, slice(128, 256), lambda t: taps - 1 - t)
+    for k in range(basis):
+        mix_t[k * chans : (k + 1) * chans, :] = mixing[k].astype(F32).T.astype(BF)
+    mid = half * rows
+    cot_t[...] = buf_c[reach, mid : mid + cells, :].astype(F32).T.astype(BF)
 
     step = LB * rows
     span = (LB + taps - 1) * rows
     n_blocks = lons // LB
 
-    def filter_all(band, buf):
-        for b in range(0, n_blocks, 2):
+    def filter_all(band, buf, begin, end):
+        for b in range(begin, end, 2):
             window = jnp.concatenate(
                 [jnp.concatenate([buf[j, (b + i) * step : (b + i) * step + span, :]
                                   for j in range(hops)], axis=0) for i in range(2)], axis=1)
@@ -218,15 +231,15 @@
     u_c = lax.broadcasted_iota(jnp.int32, (cells, cells), 1)
     unperm = ((u_r & (lons - 1)) * rows + (u_r >> lons_log) == u_c).astype(F32).astype(BF)
 
-    def pass_on(which, buf):
+    def pass_on(which, buf, part):
         for kind in (1, 2):
-            hop(which, buf, kind)[1]()
+            hop(which, buf, kind, part)[1]()
         for kind in (4, 5):
-            hop(which, buf, kind)[0]()
-
-    def wait_rest(which, buf):
+            hop(which, buf, kind, part)[0]()
+
+    def wait_rest(which, buf, part):
         for kind in (0, 3, 4, 5):
-            hop(which, buf, kind)[1]()
+            hop(which, buf, kind, part)[1]()
 
     def unpermuted(x, ref):
         ref[...] = dot(unperm, x.astype(BF)).astype(BF).reshape(ref.shape)
@@ -234,14 +247,15 @@
     stores = [pltpu.make_async_copy(src, dst, store.at[i]) for i, (src, dst) in enumerate(
         ((out, out_h), (grad_states, grad_states_h), (full, grad_mix_h)))]
 
-    pass_on(0, buf_s)
+    pass_on(0, buf_s, 0)
+    wait_rest(0, buf_s, 0)
+    filter_all(band_f, buf_s, 0, n_blocks // 2)
+    pass_on(0, buf_s, 1)
     for kind in (1, 2, 3, 0):
-        hop(1, buf_c, kind)[0]()
-    wait_rest(0, buf_s)
-    filter_all(band_f, buf_s)
-    mid = half * rows
-    cot_rows = buf_c[reach, mid : mid + cells, :]
-    grad_t = dot(cot_rows.astype(F32).T.astype(BF), filt[...])
+        hop(1, buf_c, kind, 0)[0]()
+    wait_rest(0, buf_s, 1)
+    filter_all(band_f, buf_s, n_blocks // 2, n_blocks)
+    grad_t = dot(cot_t[...], filt[...])
     for k in range(basis):
         send_a[k * chans : (k + 1) * chans, :] = grad_t[:, k * chans : (k + 1) * chans].T.astype(BF)
     piece = chunk.shape[0]
@@ -261,12 +275,9 @@
         for m in range(1, n_plane):
             a_copy(m, i).start()
 
-    pass_on(1, buf_c)
+    pass_on(1, buf_c, 0)
     unpermuted(dot(filt[...], mixing[...].reshape(basis * chans, chans)), out)
     stores[0].start()
-    build(band_a, slice(128, 256), lambda t: taps - 1 - t)
-    for k in range(basis):
-        mix_t[k * chans : (k + 1) * chans, :] = mixing[k].astype(F32).T.astype(BF)
 
     def b_copy(m, owner, i):
         return pltpu.make_async_remote_copy(
@@ -286,8 +297,8 @@
         for m in range(1, n_rest):
             b_copy(m, z, i).start()
 
-    wait_rest(1, buf_c)
-    filter_all(band_a, buf_c)
+    wait_rest(1, buf_c, 0)
+    filter_all(band_a, buf_c, 0, n_blocks)
 
     def d_copy(m, owner, i):
         return pltpu.make_async_remote_copy(
@@ -316,8 +327,9 @@
     stores[2].start()
 
     for which, buf in ((0, buf_s), (1, buf_c)):
-        for kind in range(6):
-            hop(which, buf, kind)[2]()
+        for part in range(len(halves[which])):
+            for kind in range(6):
+                hop(which, buf, kind, part)[2]()
     for i in range(PARTS):
         for m in range(1, n_plane):
             a_copy(m, i).wait_send()
@@ -331,20 +343,20 @@
 def finish(scale, out_in, grad_in, mix_in, out, grad_states, grad_mix, first, second, held, wide,
            sems):
     deep = held.shape[0]
-    cut = deep // PARTS
+    cut = deep // WRITES
     reads, writes = [], []
-    for i in range(PARTS):
+    for i in range(WRITES):
         rows = pl.ds(i * cut, cut)
         reads.append(pltpu.make_async_copy(mix_in.at[rows], held.at[rows], sems.at[0, i]))
         writes.append(pltpu.make_async_copy(wide.at[rows], grad_mix.at[rows], sems.at[1, i]))
     for i, (src, via, dst) in enumerate(((out_in, first, out), (grad_in, second, grad_states))):
-        reads.append(pltpu.make_async_copy(src, via, sems.at[0, PARTS + i]))
-        writes.append(pltpu.make_async_copy(via, dst, sems.at[1, PARTS + i]))
+        reads.append(pltpu.make_async_copy(src, via, sems.at[0, WRITES + i]))
+        writes.append(pltpu.make_async_copy(via, dst, sems.at[1, WRITES + i]))
     for copy in reads:
         copy.start()
-    for i in range(PARTS + 2):
+    for i in range(WRITES + 2):
         reads[i].wait()
-        if i < PARTS:
+        if i < WRITES:
             wide[i * cut : (i + 1) * cut, :] = held[i * cut : (i + 1) * cut, :].astype(F32) * scale
         writes[i].start()
     for copy in writes:
@@ -377,7 +389,8 @@
         ),
         in_specs=[hbm] * 11,
         out_specs=(hbm, hbm, hbm),
-        scratch_shapes=[pltpu.VMEM((rows, lons, chans), BF)] * 2 + [dma((3,))] + [pltpu.VMEM(x.shape, x.dtype) for x in operands] + [
+        scratch_shapes=[pltpu.VMEM((rows, lons, chans), BF)] * 2 + [
+            pltpu.VMEM((chans, cells), BF), dma((3,))] + [pltpu.VMEM(x.shape, x.dtype) for x in operands] + [
             dma((len(operands),)),
             pltpu.VMEM((hops, wrapped, chans), BF),
             pltpu.VMEM((hops, wrapped, chans), BF),
@@ -392,7 +405,7 @@
             pltpu.VMEM((n_rest, piece, chans), BF),
             pltpu.VMEM((piece, chans), BF),
             pltpu.VMEM((deep, chans), BF),
-            dma((2, 6)), dma((2, 6)),
+            dma((2, 6, 2)), dma((2, 6, 2)),
             dma((n_plane, PARTS)), dma((n_plane, PARTS)),
             dma((n_rest, PARTS)), dma((n_rest, PARTS)),
             dma((n_plane, PARTS)), dma((n_plane, PARTS)),
@@ -415,7 +428,7 @@
         in_specs=[hbm] * 3,
         out_specs=(hbm, hbm, hbm),
         scratch_shapes=[pltpu.VMEM((rows, lons, chans), BF)] * 2 + [
-            pltpu.VMEM((deep, chans), BF), pltpu.VMEM((deep, chans), F32), dma((2, PARTS + 2))],
+            pltpu.VMEM((deep, chans), BF), pltpu.VMEM((deep, chans), F32), dma((2, WRITES + 2))],
         compiler_params=pltpu.CompilerParams(vmem_limit_bytes=63 * 1024 * 1024),
     )(out, grad_states, grad_mix)
     shape = states.shape

time: 35.9 us -> 36.4 us (1.014)
  Pallas kernels: 35.1 us -> 35.5 us
    pallas_call x1, Pallas kernels: 33.2 us -> 33.6 us  [shards(): pl.pallas_call(functools.partial(kernel, n_dp, n_lat), out_shape=(jax.Sha...]
where the time goes in v5:
time: 36.4 us; the launch traced here: 36.2 us
  Pallas kernels  35.5 us (98%)
  between operations  0.64 us (2%)
    pallas_call x1, Pallas kernels, shards(): pl.pallas_call(functools.partial(kernel, n_dp, n_lat), out_shape=(jax.Sha...  33.6 us
    pallas_call x1, Pallas kernels, shards(): pl.pallas_call(functools.partial(finish, scale), out_shape=(jax.ShapeDtyp...  1.89 us

profile of v5, /device:TPU:0, one launch (start us, length us, event | category | flops | bytes accessed | tf_op | source)
XLA Modules:
  0.0 36.2 jit_solution(14359811450409479134)
XLA Ops:
  0.6 33.6 %shard_map.130 = (bf16[4,128,128]{2,1,0:T(8,128)(2,1)}, bf16[4,128,128]{2,1,0:T(8,128)(2,1)}, bf16[1152,128]{1,0:T(8,128)(2,1)}) custom-call(bf16[4,128,128]{2,1,0:T(8,128)(2,1)} %bitcast.12, bf16[4,128,128]{2,1,0:T(8,128)(2,1)} %bitcast.13, bf16[45,25,64]{2,1,0:T(8,128)(2,1)} %bitcast.11, s32[1,64]{1,0:T(1,128)} %bitcast.16, s32[1,64]{1,0:T(1,128)} %bitcast.17, ...), custom_call_target="tpu_custom_call" | custom-call | flops 783286272 | bytes 524288 | tf_op jit(solution)/shard_map/pallas_call | solution.py:383
  34.3 1.9 %shard_map.131 = (bf16[4,128,128]{2,1,0:T(8,128)(2,1)}, bf16[4,128,128]{2,1,0:T(8,128)(2,1)}, f32[1152,128]{1,0:T(8,128)}) custom-call(bf16[4,128,128]{2,1,0:T(8,128)(2,1)} %get-tuple-element.9.out_in, bf16[4,128,128]{2,1,0:T(8,128)(2,1)} %get-tuple-element.10.grad_in, bf16[1152,128]{1,0:T(8,128)(2,1)} %get-tuple-element.11.mix_in), custom_call_target="tpu_custom_call" | custom-call | tf_op jit(solution)/shard_map/pallas_call | solution.py:421

commit v6 on v4

--- a/solution.py
+++ b/solution.py
@@ -13,7 +13,8 @@
 LB = 4
 PLANE_DP = 2
 PLANE_LAT = 4
-PARTS = 3
+PARTS = 1
+WRITES = 3
 MESH = pl.DeviceIdType.MESH
 BF = jnp.bfloat16
 F32 = jnp.float32
@@ -186,14 +187,14 @@
     slot = place[1:2, :].astype(F32) - picked[0:1, :]
     s_i = lax.broadcasted_iota(jnp.int32, (support, 256), 0).astype(F32)
     live = jnp.where((s_i == slot) & (s_i < picked[8:9, :]), 1.0, 0.0)
-    for kt in range(basis * taps):
-        rt[kt : kt + 1, :] = jnp.sum(dot(table[kt], pick) * live, axis=0, keepdims=True)
-    entries = rt[...].astype(BF)
-
     def build(band, lanes, tap_of):
+        for kt in range(basis * taps):
+            rt[kt : kt + 1, lanes] = jnp.sum(
+                dot(table[kt], pick[:, lanes]) * live[:, lanes], axis=0, keepdims=True)
+        entries = rt[:, lanes].astype(BF)
         acc = jnp.zeros(band.shape, F32)
         for t in range(taps):
-            rows_t = (dot(expand[t], entries[:, lanes]) * own[:, lanes].astype(F32)).astype(BF)
+            rows_t = (dot(expand[t], entries) * own[:, lanes].astype(F32)).astype(BF)
             acc = acc + dot(rows_t, spread[...]) * tap[tap_of(t)].astype(F32)
         band[...] = acc.astype(BF)
 
@@ -213,10 +214,6 @@
                 for k in range(basis):
                     filt[(b + i) * step : (b + i + 1) * step, k * chans : (k + 1) * chans] = (
                         res[k * step : (k + 1) * step, i * chans : (i + 1) * chans])
-
-    u_r = lax.broadcasted_iota(jnp.int32, (cells, cells), 0)
-    u_c = lax.broadcasted_iota(jnp.int32, (cells, cells), 1)
-    unperm = ((u_r & (lons - 1)) * rows + (u_r >> lons_log) == u_c).astype(F32).astype(BF)
 
     def pass_on(which, buf):
         for kind in (1, 2):
@@ -261,6 +258,9 @@
         for m in range(1, n_plane):
             a_copy(m, i).start()
 
+    u_r = lax.broadcasted_iota(jnp.int32, (cells, cells), 0)
+    u_c = lax.broadcasted_iota(jnp.int32, (cells, cells), 1)
+    unperm = ((u_r & (lons - 1)) * rows + (u_r >> lons_log) == u_c).astype(F32).astype(BF)
     pass_on(1, buf_c)
     unpermuted(dot(filt[...], mixing[...].reshape(basis * chans, chans)), out)
     stores[0].start()
@@ -331,20 +331,20 @@
 def finish(scale, out_in, grad_in, mix_in, out, grad_states, grad_mix, first, second, held, wide,
            sems):
     deep = held.shape[0]
-    cut = deep // PARTS
+    cut = deep // WRITES
     reads, writes = [], []
-    for i in range(PARTS):
+    for i in range(WRITES):
         rows = pl.ds(i * cut, cut)
         reads.append(pltpu.make_async_copy(mix_in.at[rows], held.at[rows], sems.at[0, i]))
         writes.append(pltpu.make_async_copy(wide.at[rows], grad_mix.at[rows], sems.at[1, i]))
     for i, (src, via, dst) in enumerate(((out_in, first, out), (grad_in, second, grad_states))):
-        reads.append(pltpu.make_async_copy(src, via, sems.at[0, PARTS + i]))
-        writes.append(pltpu.make_async_copy(via, dst, sems.at[1, PARTS + i]))
+        reads.append(pltpu.make_async_copy(src, via, sems.at[0, WRITES + i]))
+        writes.append(pltpu.make_async_copy(via, dst, sems.at[1, WRITES + i]))
     for copy in reads:
         copy.start()
-    for i in range(PARTS + 2):
+    for i in range(WRITES + 2):
         reads[i].wait()
-        if i < PARTS:
+        if i < WRITES:
             wide[i * cut : (i + 1) * cut, :] = held[i * cut : (i + 1) * cut, :].astype(F32) * scale
         writes[i].start()
     for copy in writes:
@@ -415,7 +415,7 @@
         in_specs=[hbm] * 3,
         out_specs=(hbm, hbm, hbm),
         scratch_shapes=[pltpu.VMEM((rows, lons, chans), BF)] * 2 + [
-            pltpu.VMEM((deep, chans), BF), pltpu.VMEM((deep, chans), F32), dma((2, PARTS + 2))],
+            pltpu.VMEM((deep, chans), BF), pltpu.VMEM((deep, chans), F32), dma((2, WRITES + 2))],
         compiler_params=pltpu.CompilerParams(vmem_limit_bytes=63 * 1024 * 1024),
     )(out, grad_states, grad_mix)
     shape = states.shape

time: 35.9 us -> 35 us (0.975)
  Pallas kernels: 35.1 us -> 34.2 us
    pallas_call x1, Pallas kernels: 33.2 us -> 32.3 us  [shards(): pl.pallas_call(functools.partial(kernel, n_dp, n_lat), out_shape=(jax.Sha...]
where the time goes in v6:
time: 35 us; the launch traced here: 34.8 us
  Pallas kernels  34.2 us (98%)
  between operations  0.64 us (2%)
    pallas_call x1, Pallas kernels, shards(): pl.pallas_call(functools.partial(kernel, n_dp, n_lat), out_shape=(jax.Sha...  32.3 us
    pallas_call x1, Pallas kernels, shards(): pl.pallas_call(functools.partial(finish, scale), out_shape=(jax.ShapeDtyp...  1.89 us

profile of v6, /device:TPU:0, one launch (start us, length us, event | category | flops | bytes accessed | tf_op | source)
XLA Modules:
  0.0 34.8 jit_solution(2262460098020774682)
XLA Ops:
  0.6 32.3 %shard_map.130 = (bf16[4,128,128]{2,1,0:T(8,128)(2,1)}, bf16[4,128,128]{2,1,0:T(8,128)(2,1)}, bf16[1152,128]{1,0:T(8,128)(2,1)}) custom-call(bf16[4,128,128]{2,1,0:T(8,128)(2,1)} %bitcast.12, bf16[4,128,128]{2,1,0:T(8,128)(2,1)} %bitcast.13, bf16[45,25,64]{2,1,0:T(8,128)(2,1)} %bitcast.11, s32[1,64]{1,0:T(1,128)} %bitcast.16, s32[1,64]{1,0:T(1,128)} %bitcast.17, ...), custom_call_target="tpu_custom_call" | custom-call | flops 783286272 | bytes 524288 | tf_op jit(solution)/shard_map/pallas_call | solution.py:371
  32.9 1.9 %shard_map.131 = (bf16[4,128,128]{2,1,0:T(8,128)(2,1)}, bf16[4,128,128]{2,1,0:T(8,128)(2,1)}, f32[1152,128]{1,0:T(8,128)}) custom-call(bf16[4,128,128]{2,1,0:T(8,128)(2,1)} %get-tuple-element.9.out_in, bf16[4,128,128]{2,1,0:T(8,128)(2,1)} %get-tuple-element.10.grad_in, bf16[1152,128]{1,0:T(8,128)(2,1)} %get-tuple-element.11.mix_in), custom_call_target="tpu_custom_call" | custom-call | tf_op jit(solution)/shard_map/pallas_call | solution.py:408
